TPU v7x, 128 devices: a whole 4x4x4 slice. The times are simulated.
128 devices in a mesh: box: 32 (over y, z, core), node: 4 (over x).
Axes of the slice: x: 4, y: 4, z: 4, core: 2. Of those that a mesh axis runs over, the one named last changes fastest.
Arguments:
- fine_rhs: float32 [1024, 32, 1024], P(('box', 'node')), may hold values from -6 to 6
- fine_diag: float32 [1024, 32, 1024], P(('box', 'node')), may hold values from 0.25 to 4
- fine_count: int32 [32, 4], P('box', 'node'), may hold values from 1 to 8, as said below
- fine_nbr: int32 [1024, 6], P(('box', 'node')), may hold values from -1 to 23, as said below
- fine_cover: int32 [32, 32], P('box', 'node'), may hold values from 0 to 31, each once within a row
- coarse_source: float32 [128, 32, 1024], P(('box', 'node')), may hold values from -6 to 6
- coarse_diag: float32 [128, 32, 1024], P(('box', 'node')), may hold values from 0.25 to 4
- coarse_nbr: int32 [128, 6], P(('box', 'node')), may hold values from -1 to 2, as said below
- coarse_place: int32 [128], P(('box', 'node')), may hold values from 0 to 32767, as said below
- bottom_diag: float32 [256, 256, 256], P('box', 'node'), may hold values from 0.1 to 6
Outputs:
- fine_correction: float32 [1024, 32, 1024], P(('box', 'node'))
- coarse_correction: float32 [128, 32, 1024], P(('box', 'node'))
Inputs may be any that keep to these rules, and one draw needn't show every extreme that they name: `fine_count`: the first that many slots of a device hold boxes; some device holds 8. `fine_nbr`: entry w indexes the boxes of the device before, this device and the device after, 8 each in that order; -1 where no fine box lies across the face. Empty slots have -1 throughout; no entry names an empty slot or a device beyond the ends. `fine_cover`: within a group of 4 devices along node, v // 8 counts the group's middle boxes in node order; every pair of box and octant is named once. `coarse_nbr`: as for fine_nbr with 1 boxes a device; every slot holds a box. `coarse_place`: no two middle boxes share a block; some middle box takes the last block.
All inputs are finite; a program needn't handle non-finite values.
Results may differ from a plain program's by a relative error of at most 0.00002.
Values sent between devices are 32-bit elements; how exact they have to be, the bound alone decides.
A program may use at most 128 MiB of HBM per device.

v0:
```python
import jax
import jax.numpy as jnp
from jax import lax
from jax.sharding import PartitionSpec as P

BOT_ITERS = 12


relax = 0.8
opposite_faces = (1, 0, 3, 2, 5, 4)


def padded_2(shard, sides, width):
    for axis, dim in sides:
        size, length = (lax.axis_size(axis), shard.shape[dim])
        up = [(i, (i + 1) % size) for i in range(size - 1)]
        down = [(j, i) for i, j in up]
        last = lax.slice_in_dim(shard, length - width, length, axis=dim)
        leading = lax.slice_in_dim(shard, 0, width, axis=dim)
        before = lax.ppermute(last, axis, up)
        after = lax.ppermute(leading, axis, down)
        shard = jnp.concatenate([before, shard, after], axis=dim)
    return shard


def shift_sum(current, low_x, high_x, low_y, high_y, low_z, high_z):
    edge_len = low_y.shape[2]
    plane_len = current.shape[2]
    along_x = jnp.concatenate([low_x, current[:, :-1]], 1) + jnp.concatenate(
        [current[:, 1:], high_x], 1
    )
    along_y = jnp.concatenate([low_y, current[:, :, :-edge_len]], 2) + jnp.concatenate(
        [current[:, :, edge_len:], high_y], 2
    )
    column = jnp.arange(plane_len, dtype=jnp.int32) % edge_len
    below_z = jnp.where(
        column == 0,
        jnp.repeat(low_z, edge_len, axis=2),
        jnp.concatenate([current[:, :, :1], current[:, :, :-1]], 2),
    )
    above_z = jnp.where(
        column == edge_len - 1,
        jnp.repeat(high_z, edge_len, axis=2),
        jnp.concatenate([current[:, :, 1:], current[:, :, -1:]], 2),
    )
    return along_x + along_y + below_z + above_z


def box_sum(current, ghosts):
    box_count, edge_len, plane_len = current.shape

    def face_of(face_no):
        return ghosts[:, face_no].reshape(box_count, edge_len, edge_len)

    return shift_sum(
        current, ghosts[:, 0:1], ghosts[:, 1:2], face_of(2), face_of(3), face_of(4), face_of(5)
    )


def box_faces(current):
    box_count, edge_len, plane_len = current.shape
    return jnp.stack(
        [
            current[:, 0],
            current[:, edge_len - 1],
            current[:, :, :edge_len].reshape(box_count, plane_len),
            current[:, :, plane_len - edge_len :].reshape(box_count, plane_len),
            current[:, :, 0::edge_len].reshape(box_count, plane_len),
            current[:, :, edge_len - 1 :: edge_len].reshape(box_count, plane_len),
        ],
        1,
    )


def pick_ghosts(window, nbr_lists):
    window_len = window.shape[0]
    chosen = window[
        jnp.clip(nbr_lists, 0, window_len - 1), jnp.array(opposite_faces, dtype=jnp.int32)[None, :]
    ]
    return jnp.where((nbr_lists >= 0)[:, :, None], chosen, 0.0)


def relax_first(source, diagonal):
    return relax * (source / (6.0 + diagonal))


def relax_again(current, source, diagonal, beside_all):
    image_sum = (6.0 + diagonal) * current - beside_all
    return current + relax * ((source - image_sum) / (6.0 + diagonal))


def residual_of(current, source, diagonal, beside_all):
    return source - ((6.0 + diagonal) * current - beside_all)


def coarsen(current, factor, weight_scale):
    box_count, edge_len, plane_len = current.shape
    small_len = edge_len // factor
    shaped = current.reshape(box_count, small_len, factor, small_len, factor, small_len, factor)
    return shaped.sum(axis=(2, 4, 6)) * weight_scale


def refine(pieces, factor):
    box_count, small_len = (pieces.shape[0], pieces.shape[1])
    grown = jnp.repeat(
        jnp.repeat(jnp.repeat(pieces, factor, axis=1), factor, axis=2), factor, axis=3
    )
    return grown.reshape(box_count, small_len * factor, (small_len * factor) ** 2)


def to_octants(current):
    box_count, edge_len, plane_len = current.shape
    half_len = edge_len // 2
    shaped = current.reshape(box_count, 2, half_len, 2, half_len, 2, half_len)
    return shaped.transpose(0, 1, 3, 5, 2, 4, 6).reshape(
        box_count * 8, half_len, half_len, half_len
    )


def from_octants(pieces):
    half_len = pieces.shape[1]
    box_count = pieces.shape[0] // 8
    shaped = pieces.reshape(box_count, 2, 2, 2, half_len, half_len, half_len)
    return shaped.transpose(0, 1, 4, 2, 5, 3, 6).reshape(
        box_count, 2 * half_len, 4 * half_len * half_len
    )


def shards(
    fine_rhs,
    fine_diag,
    fine_count,
    fine_nbr,
    fine_cover,
    coarse_source,
    coarse_diag,
    coarse_nbr,
    coarse_place,
    bottom_diag,
):
    fine_total, edge_len, plane_len = fine_rhs.shape
    coarse_total = coarse_source.shape[0]
    node_count = lax.axis_size("node")
    half_len = edge_len // 2
    quarter = edge_len // 4
    is_live = jnp.arange(fine_total, dtype=jnp.int32) < fine_count.reshape(-1)[0]
    cover = fine_cover.reshape(-1)

    def fine_around(current):
        window = padded_2(box_faces(current), ((("box", "node"), 0),), fine_total)
        return box_sum(current, pick_ghosts(window, fine_nbr))

    def coarse_around(current):
        window = padded_2(box_faces(current), ((("box", "node"), 0),), coarse_total)
        return box_sum(current, pick_ghosts(window, coarse_nbr))

    fine = relax_first(fine_rhs, fine_diag)
    fine = relax_again(fine, fine_rhs, fine_diag, fine_around(fine))
    fine_res = jnp.where(
        is_live[:, None, None], residual_of(fine, fine_rhs, fine_diag, fine_around(fine)), 0.0
    )
    octants = coarsen(fine_res, 2, 0.5)
    placed = (
        jnp.zeros((node_count * coarse_total * 8, half_len, half_len, half_len), jnp.float32)
        .at[cover]
        .set(octants)
    )
    lifted = lax.psum_scatter(from_octants(placed), "node", scatter_dimension=0, tiled=True)
    coarse_rhs = coarse_source + lifted
    coarse = relax_first(coarse_rhs, coarse_diag)
    coarse = relax_again(coarse, coarse_rhs, coarse_diag, coarse_around(coarse))
    coarse_res = residual_of(coarse, coarse_rhs, coarse_diag, coarse_around(coarse))
    blocks = coarsen(coarse_res, 4, 0.25).reshape(coarse_total, quarter, quarter * quarter)
    all_blocks, all_places = (
        lax.all_gather(blocks, ("box", "node"), axis=0, tiled=True),
        lax.all_gather(coarse_place, ("box", "node"), axis=0, tiled=True),
    )
    rows_x, rows_y, grid_len = bottom_diag.shape
    per_side = grid_len // quarter
    slab_bx = rows_x // quarter
    slab_by = rows_y // quarter
    slab_blocks = slab_bx * slab_by * per_side
    blocks_all = all_blocks.reshape(-1, quarter, quarter, quarter)
    block_x = all_places // (per_side * per_side)
    block_y = all_places // per_side % per_side
    block_z = all_places % per_side
    first_bx = lax.axis_index("box") * slab_bx
    first_by = lax.axis_index("node") * slab_by
    inside = (
        (block_x >= first_bx)
        & (block_x < first_bx + slab_bx)
        & (block_y >= first_by)
        & (block_y < first_by + slab_by)
    )
    local_no = jnp.where(
        inside,
        ((block_x - first_bx) * slab_by + (block_y - first_by)) * per_side + block_z,
        slab_blocks,
    )
    local_no = local_no.astype(jnp.int32)
    slab_parts = (
        jnp.zeros((slab_blocks, quarter, quarter, quarter), jnp.float32)
        .at[local_no]
        .set(blocks_all, mode="drop")
    )
    slab_rhs = (
        slab_parts.reshape(slab_bx, slab_by, per_side, quarter, quarter, quarter)
        .transpose(0, 3, 1, 4, 2, 5)
        .reshape(rows_x, rows_y, grid_len)
    )

    def sweep_slab(sweep_no, current):
        padded = padded_2(current, (("box", 0), ("node", 1)), 1)
        zero_col = jnp.zeros((rows_x, rows_y, 1), jnp.float32)
        along_z = jnp.concatenate([zero_col, current[:, :, :-1]], 2) + jnp.concatenate(
            [current[:, :, 1:], zero_col], 2
        )
        beside_all = (
            padded[2:, 1:-1] + padded[:-2, 1:-1] + padded[1:-1, 2:] + padded[1:-1, :-2] + along_z
        )
        return relax_again(current, slab_rhs, bottom_diag, beside_all)

    solved = lax.fori_loop(0, BOT_ITERS - 1, sweep_slab, relax_first(slab_rhs, bottom_diag))
    solved_parts = (
        solved.reshape(slab_bx, quarter, slab_by, quarter, per_side, quarter)
        .transpose(0, 2, 4, 1, 3, 5)
        .reshape(slab_blocks, quarter, quarter, quarter)
    )
    picked = solved_parts[jnp.clip(local_no, 0, slab_blocks - 1)]
    picked = jnp.where(inside[:, None, None, None], picked, 0.0)
    summed = lax.psum(picked, ("box", "node"))
    device_no = lax.axis_index("box") * node_count + lax.axis_index("node")
    own_blocks = lax.dynamic_slice_in_dim(summed, device_no * coarse_total, coarse_total, 0)
    coarse = coarse + refine(own_blocks, 4)
    for sweep_no in range(2):
        coarse = relax_again(coarse, coarse_rhs, coarse_diag, coarse_around(coarse))
    group_coarse = lax.all_gather(coarse, "node", axis=0, tiled=True)
    fine = fine + refine(to_octants(group_coarse)[cover], 2)
    for sweep_no in range(2):
        fine = relax_again(fine, fine_rhs, fine_diag, fine_around(fine))
    return (jnp.where(is_live[:, None, None], fine, 0.0), coarse)


def solution(mesh):
    return jax.shard_map(
        shards,
        mesh=mesh,
        in_specs=(
            P(("box", "node"), None, None),
            P(("box", "node"), None, None),
            P("box", "node"),
            P(("box", "node"), None),
            P("box", "node"),
            P(("box", "node"), None, None),
            P(("box", "node"), None, None),
            P(("box", "node"), None),
            P(("box", "node")),
            P("box", "node", None),
        ),
        out_specs=(P(("box", "node"), None, None), P(("box", "node"), None, None)),
        check_vma=False,
    )
```

profile of v0, /device:TPU:0, one launch (start us, length us, event | category | flops | bytes accessed | tf_op | source)
XLA Modules:
  0.0 972.6 jit_solution(16692492205516734228)
XLA Ops:
  26.3 69.1 %all-reduce.2 = s32[128]{0:T(128)S(1)} all-reduce(s32[128]{0:T(128)S(1)} %dynamic-update-slice), channel_id=1, replica_groups=mesh['box'=32,'node'=4] {'box','node'}, use_global_device_ids=true, to_apply=%add.2 | all-reduce | flops 128 | bytes 1024
  101.3 4.6 reshape.1304
  108.7 4.6 reshape.1305
  113.6 6.0 multiply_add_fusion.1
  153.1 4.6 reshape.1307
  162.0 4.6 reshape.1308
  170.1 7.0 fusion.20
  177.1 9.3 copy.294
  186.4 12.4 %reduce_sum.18 = f32[8,16,16,16]{0,3,2,1:T(8,128)S(1)} reduce(f32[8,16,2,16,2,16,2]{0,6,5,4,3,2,1:T(2,128)} %bitcast.114, f32[]{:T(128)} %constant.123.clone.1), dimensions={2,4,6}, to_apply=%region_0.1 | reduce | flops 229376 | bytes 1179652 | tf_op jit(solution)/shard_map/reduce_sum | solution.py:100
  207.1 7.5 copy.296
  214.6 8.8 reshape.1311
  224.8 23.0 %reduce-scatter.2.cloned.1.call-done = f32[1,32,1024]{2,1,0:T(8,128)} async-done(((f32[4,32,1024]{2,1,0:T(8,128)}), f32[1,32,1024]{2,1,0:T(8,128)}) %reduce-scatter.2.cloned.1.call-update) | async-done | bytes 131088 | tf_op jit(solution)/shard_map/reduce_scatter | solution.py:168
  271.7 5.7 reshape.1312
  280.0 62.9 %all_gather.10 = f32[128,8,64]{2,1,0:T(8,128)S(1)} all-gather(f32[1,8,64]{2,1,0:T(8,128)S(1)} %mul.113), channel_id=1, replica_groups=mesh['box'=32,'node'=4] {'box','node'}, dimensions={0}, use_global_device_ids=true | all-gather | bytes 264192 | tf_op jit(solution)/shard_map/all_gather | solution.py:175
  343.0 4.6 copy.298
  352.0 20.7 %scatter_fusion.1 = f32[256,8,8,8]{3,2,1,0:T(8,128)} fusion(f32[256,8,8,8]{3,2,1,0:T(8,128)} %broadcast_in_dim.320, s32[128]{0:T(128)S(1)} %compare_select_fusion.2, f32[128,8,8,8]{3,2,1,0:T(8,128)} %copy.298), kind=kCustom, calls=%fused_computation.11 | custom fusion | bytes 786944 | tf_op jit(solution)/shard_map/scatter | solution.py:204
  372.8 6.4 copy.329
  379.2 4.8 copy.300
  383.9 6.9 reshape.1315
  392.8 228.6 %while.10 = (s32[]{:T(128)}, f32[8,64,256]{2,1,0:T(8,128)}, f32[8,64,256]{2,1,0:T(8,128)}, f32[8,64,256]{2,1,0:T(8,128)S(1)}, s32[]{:T(128)}) while((s32[]{:T(128)}, f32[8,64,256]{2,1,0:T(8,128)}, f32[8,64,256]{2,1,0:T(8,128)}, f32[8,64,256]{2,1,0:T(8,128)S(1)}, s32[]{:T(128)}) %tuple.127), condition=%wide.region_6.7_spmd, body=%wide.region_5.6_spmd.sunk | while | flops 2097154 | bytes 11927801 | solution.py:223
  402.4 4.4 collective-permute-done.3
  422.4 4.4 collective-permute-done.3
  443.1 4.4 collective-permute-done.3
  462.9 4.4 collective-permute-done.3
  482.8 4.4 collective-permute-done.3
  490.9 4.9 collective-permute-start
  504.3 4.4 collective-permute-done.3
  512.3 5.7 collective-permute-start
  526.4 4.4 collective-permute-done.3
  534.5 5.6 collective-permute-start
  548.5 4.4 collective-permute-done.3
  556.5 5.5 collective-permute-start
  578.5 5.5 collective-permute-start
  600.5 5.5 collective-permute-start
  621.4 7.3 reshape.1316
  628.7 11.4 %copy.330 = f32[1,8,32,8,8,8]{5,4,3,2,1,0:T(8,128)} copy(f32[1,8,32,8,8,8]{5,2,4,1,3,0:T(8,128)} %bitcast.116) | data formatting | bytes 1048576 | tf_op jit(solution)/shard_map/reshape | solution.py:227
  640.1 6.4 gather_fusion.4
  646.5 4.6 broadcast_select_fusion
  651.1 167.2 %all-reduce.5.cloned.1.call-done = f32[128,8,8,8]{3,2,1,0:T(8,128)} async-done(((f32[128,8,8,8]{3,2,1,0:T(8,128)}), f32[128,8,8,8]{3,2,1,0:T(8,128)}) %all-reduce.5.cloned.1.call-update) | async-done | bytes 262160 | tf_op jit(solution)/shard_map/psum | solution.py:231
  844.0 13.4 %all_gather.11 = f32[4,32,1024]{2,1,0:T(8,128)S(1)} all-gather(f32[1,32,1024]{2,1,0:T(8,128)S(1)} %multiply_add_fusion.2), channel_id=1, replica_groups=mesh['box'=32,'node'=4] {'node'}, dimensions={0}, use_global_device_ids=true | all-gather | bytes 655360 | tf_op jit(solution)/shard_map/all_gather | solution.py:237
  857.4 7.5 reshape.1318
  864.8 4.7 copy.305
  902.5 4.6 reshape.1322
  909.8 4.6 reshape.1323
  914.8 6.5 multiply_add_fusion
  941.8 4.6 reshape.1324
  949.1 4.6 reshape.1325
  958.0 6.0 add_select_fusion
  (574 shorter events, 360.6 us)
Async XLA Ops:
  7.2 240.6 %reduce-scatter.2.cloned.1.call-start = ((), (), s32[]{:S(2)}) async-start(), calls=%async_computation.1 | async-start | bytes 655360 | tf_op jit(solution)/shard_map/reduce_scatter | solution.py:168
  13.4 83.2 %collective-permute-start.4 = (f32[8,6,1024]{2,0,1:T(8,128)S(1)}, f32[8,6,1024]{2,0,1:T(8,128)S(1)}, u32[]{:S(2)}, u32[]{:S(2)}) collective-permute-start(f32[8,6,1024]{2,0,1:T(8,128)S(1)} %constant_dynamic-update-slice_fusion.3), channel_id=1, source_target_pairs={{0,1},{1,2},{2,3},{3,4},{4,5},{5,6},{6,7},{7,8},{8,9},{9,10},{10,1... | collective-permute-start | bytes 589832 | tf_op jit(solution)/shard_map/ppermute | solution.py:20
  16.9 79.7 %collective-permute-start.5 = (f32[8,6,1024]{2,0,1:T(8,128)S(1)}, f32[8,6,1024]{2,0,1:T(8,128)S(1)}, u32[]{:S(2)}, u32[]{:S(2)}) collective-permute-start(f32[8,6,1024]{2,0,1:T(8,128)S(1)} %constant_dynamic-update-slice_fusion.3), channel_id=1, source_target_pairs={{1,0},{2,1},{3,2},{4,3},{5,4},{6,5},{7,6},{8,7},{9,8},{10,9},{11,1... | collective-permute-start | bytes 589832 | tf_op jit(solution)/shard_map/ppermute | solution.py:21
  131.8 9.6 collective-permute-start.6
  134.6 8.2 collective-permute-start.7
  223.4 594.9 %all-reduce.5.cloned.1.call-start = ((), (), s32[]{:S(2)}) async-start(), calls=%async_computation.2 | async-start | bytes 8388608 | tf_op jit(solution)/shard_map/psum | solution.py:231
  251.0 5.8 collective-permute-start.9
  259.8 5.5 collective-permute-start.10
  263.7 5.8 collective-permute-start.11
  400.9 5.9 collective-permute-start.3
  412.6 4.0 collective-permute-start.1
  417.3 5.1 collective-permute-start.2
  420.9 5.9 collective-permute-start.3
  430.5 4.7 collective-permute-start
  433.9 4.0 collective-permute-start.1
  438.7 4.4 collective-permute-start.2
  441.6 5.9 collective-permute-start.3
  451.1 4.7 collective-permute-start
  454.6 4.0 collective-permute-start.1
  461.4 5.9 collective-permute-start.3
  471.0 4.8 collective-permute-start
  481.3 5.9 collective-permute-start.3
  490.9 6.2 collective-permute-start
  495.8 4.1 collective-permute-start.1
  502.8 5.9 collective-permute-start.3
  512.3 7.0 collective-permute-start
  518.1 4.0 collective-permute-start.1
  524.9 5.9 collective-permute-start.3
  534.5 6.9 collective-permute-start
  540.1 4.0 collective-permute-start.1
  546.9 5.9 collective-permute-start.3
  556.5 6.8 collective-permute-start
  562.1 4.0 collective-permute-start.1
  568.9 5.9 collective-permute-start.3
  578.5 6.8 collective-permute-start
  584.0 4.0 collective-permute-start.1
  590.9 5.9 collective-permute-start.3
  600.5 6.8 collective-permute-start
  606.0 4.0 collective-permute-start.1
  612.9 5.9 collective-permute-start.3
  820.4 4.9 collective-permute-start.12
  823.7 5.8 collective-permute-start.13
  832.5 5.1 collective-permute-start.14
  836.0 5.8 collective-permute-start.15
  887.5 8.0 collective-permute-start.16
  889.1 8.5 collective-permute-start.17
  924.7 9.4 collective-permute-start.18
  927.6 9.2 collective-permute-start.19
  (56 other events, 959.7 us)
Sparse Core Ops, SparseCore 0:
  223.5 24.2 reduce-scatter.1
  651.2 167.0 all-reduce.4
where the time goes:
time: 992 us; the launch traced here: 973 us
  local copies, waits for them, and re-layouts  298 us (30%)
  waiting for transfers between devices  290 us (29%)
  blocking collectives  145 us (15%)
  starting transfers between devices  133 us (13%)
  other arithmetic  88.5 us (9%)
  between operations  17.1 us (2%)
    psum x1, waiting for transfers between devices, shards(): summed = lax.psum(picked, ('box', 'node'))  167 us
    ppermute x30, waiting for transfers between devices, padded_2(): after = lax.ppermute(leading, axis, down)  99.4 us
    ppermute x30, starting transfers between devices, padded_2(): before = lax.ppermute(last, axis, up)  94.5 us
    unnamed x1, blocking collectives  69.1 us
    all_gather x1, blocking collectives, shards(): lax.all_gather(blocks, ('box', 'node'), axis=0, tiled=True)  62.9 us
    add x16, other arithmetic, relax_again(): return current + relax * ((source - image_sum) / (6.0 + diagonal))  42.3 us
    ppermute x30, starting transfers between devices, padded_2(): after = lax.ppermute(leading, axis, down)  38.6 us
    reduce_scatter x1, waiting for transfers between devices, shards(): lax.psum_scatter(from_octants(placed), 'node', scatter_dimension=0, tiled...  23 us
  transfers between devices with their start and end apart: 62, of which 31 were waited for; matrix products, arithmetic and copies ran while one was open for 3% of the time, Pallas kernels for 0%

commit v1 on v0

v1 whole, which is shorter than its diff:
```python
import functools

import jax
import jax.numpy as jnp
from jax import lax
from jax.experimental import pallas as pl
from jax.experimental.pallas import tpu as pltpu
from jax.sharding import PartitionSpec as P

F32, BF16, I32 = jnp.float32, jnp.bfloat16, jnp.int32
MESH = pl.DeviceIdType.MESH
BOT_ITERS = 12
HALO = BOT_ITERS - 1
Y_HALO = 16
TILES = 8


def grid_of(n_box):
    return {32: (4, 4, 2), 8: (2, 2, 2)}[n_box]


def lanes_of(shape):
    return lax.broadcasted_iota(I32, shape, len(shape) - 1)


def rows_of(shape):
    return lax.broadcasted_iota(I32, shape, len(shape) - 2)


def thirds(a):
    high = a.astype(BF16)
    rest = a - high.astype(F32)
    middle = rest.astype(BF16)
    low = (rest - middle.astype(F32)).astype(BF16)
    return high, middle, low


def pick_right(a, one_hot):
    high, middle, low = [jnp.dot(t, one_hot, preferred_element_type=F32) for t in thirds(a)]
    return high + (middle + low)


def pick_left(one_hot, a):
    high, middle, low = [jnp.dot(one_hot, t, preferred_element_type=F32) for t in thirds(a)]
    return high + (middle + low)


def one_hot_of(shape, test):
    return jnp.where(test(rows_of(shape), lanes_of(shape)), 1.0, 0.0).astype(BF16)


def roll_lanes(a, shift):
    shift = shift % 128
    return a if shift == 0 else pltpu.roll(a, shift, 1)


def tiles_of(ref, box):
    return [ref[box, :, 128 * t : 128 * (t + 1)] for t in range(TILES)]


def pack_faces(tiles):
    lane = lanes_of((32, 128))
    within, quarter = lane % 32, lane // 32
    first, last = tiles[0], tiles[-1]
    packed = jnp.where(
        quarter == 0,
        first,
        jnp.where(
            quarter == 1,
            jnp.where(within < 16, roll_lanes(first, 40), roll_lanes(first, 24)),
            jnp.where(
                quarter == 2,
                jnp.where(within < 16, roll_lanes(last, -24), roll_lanes(last, -40)),
                last,
            ),
        ),
    )
    for t in range(TILES):
        packed = jnp.where(within == t, roll_lanes(tiles[t], t), packed)
        packed = jnp.where(within == 31 - t, roll_lanes(tiles[t], -t), packed)
    return packed


def put_faces(tiles, yz_ref, x_ref, slot):
    yz_ref[slot] = pack_faces(tiles)
    for t in range(TILES):
        x_ref[slot, 0:1, 128 * t : 128 * (t + 1)] = tiles[t][0:1, :]
        x_ref[slot, 1:2, 128 * t : 128 * (t + 1)] = tiles[t][31:32, :]


def ghosts_of(yz_ref, x_ref, nbr_ref, box):
    def chosen(ref, face):
        which = nbr_ref[box, face]
        kept = jnp.where(which >= 0, 1.0, 0.0).astype(F32)
        return ref[jnp.maximum(which, 0)], kept

    def tile(face):
        value, kept = chosen(yz_ref, face)
        return value * kept

    x_low, low_kept = chosen(x_ref, 0)
    x_high, high_kept = chosen(x_ref, 1)
    return (
        x_low[1:2] * low_kept,
        x_high[0:1] * high_kept,
        tile(2),
        tile(3),
        tile(4),
        tile(5),
    )


def beside(tiles, ghosts):
    x_low, x_high, y_low, y_high, z_low, z_high = ghosts
    lane, row = lanes_of((32, 128)), rows_of((32, 128))
    within = lane % 32
    below = jnp.where(
        within < 8,
        roll_lanes(y_low, 56),
        jnp.where(within < 24, roll_lanes(y_low, 32), roll_lanes(y_low, 72)),
    )
    above = jnp.where(
        within < 8,
        roll_lanes(y_high, 56),
        jnp.where(within < 24, roll_lanes(y_high, 96), roll_lanes(y_high, 72)),
    )
    ups = [below] + [roll_lanes(t, 32) for t in tiles]
    downs = [roll_lanes(t, 96) for t in tiles] + [above]
    sums = []
    for t in range(TILES):
        cut = slice(128 * t, 128 * (t + 1))
        along_x = jnp.where(row == 0, x_low[:, cut], pltpu.roll(tiles[t], 1, 0)) + jnp.where(
            row == 31, x_high[:, cut], pltpu.roll(tiles[t], 31, 0)
        )
        along_y = jnp.where(lane < 32, ups[t], ups[t + 1]) + jnp.where(
            lane >= 96, downs[t + 1], downs[t]
        )
        along_z = jnp.where(
            within == 0, roll_lanes(z_low, t - 31), roll_lanes(tiles[t], 1)
        ) + jnp.where(within == 31, roll_lanes(z_high, 31 - t), roll_lanes(tiles[t], 127))
        sums.append(along_x + along_y + along_z)
    return sums


class Copies:
    def __init__(self, send_sems, recv_sems):
        self.send_sems, self.recv_sems, self.made = send_sems, recv_sems, []

    def start(self, source, target, device):
        number = len(self.made)
        copy = pltpu.make_async_remote_copy(
            src_ref=source,
            dst_ref=target,
            send_sem=self.send_sems.at[number],
            recv_sem=self.recv_sems.at[number],
            device_id=device,
            device_id_type=MESH,
        )
        copy.start()
        self.made.append(copy)
        return copy

    def finish(self):
        for copy in self.made:
            copy.wait_send()


def arrived(copies):
    for copy in copies:
        copy.wait_recv()


class Place:
    def __init__(self, n_box, n_node):
        self.n_box, self.n_node = n_box, n_node
        self.ny, self.nz, self.nc = grid_of(n_box)
        self.box, self.node = lax.axis_index("box"), lax.axis_index("node")
        self.core = self.box % self.nc
        self.z = self.box // self.nc % self.nz
        self.y = self.box // (self.nc * self.nz)

    def along_line(self, step):
        total = self.n_box * self.n_node
        other = (self.box * self.n_node + self.node + step + total) % total
        return (other // self.n_node, other % self.n_node)

    def next_node(self, step):
        return (self.node + step + self.n_node) % self.n_node

    def at_node(self, step):
        return (self.box, self.next_node(step))

    def at_box(self, step):
        return ((self.box + step + self.n_box) % self.n_box, self.node)

    def in_box(self, y, z, core):
        return ((y * self.nz + z) * self.nc + core, self.node)

    def peers_y(self):
        for step in range(1, self.ny):
            other = (self.y + step) % self.ny
            yield other, self.in_box(other, self.z, self.core)

    def peers_z(self):
        for step in range(1, self.nz):
            other = (self.z + step) % self.nz
            yield other, self.in_box(self.y, other, self.core)

    def peer_core(self):
        other = 1 - self.core
        return other, self.in_box(self.y, self.z, other)

    def peers_node(self):
        for step in range(1, self.n_node):
            yield self.next_node(step), self.at_node(step)

    def barrier(self, more):
        peers = [self.along_line(1), self.along_line(-1)] + more
        for peers_of in (self.peers_node, self.peers_y, self.peers_z):
            peers += [device for _, device in peers_of()]
        peers.append(self.peer_core()[1])
        barrier = pltpu.get_barrier_semaphore()
        for device in peers:
            pl.semaphore_signal(barrier, inc=1, device_id=device, device_id_type=MESH)
        pl.semaphore_wait(barrier, len(peers))


def send_faces(copies, here, yz_ref, x_ref, count):
    own, before, after = (pl.ds(count, count), pl.ds(0, count), pl.ds(2 * count, count))
    started = []
    for ref in (yz_ref, x_ref):
        started.append(copies.start(ref.at[own], ref.at[before], here.along_line(1)))
        started.append(copies.start(ref.at[own], ref.at[after], here.along_line(-1)))
    return started


def write_tiles(ref, box, tiles):
    for t in range(TILES):
        ref[box, :, 128 * t : 128 * (t + 1)] = tiles[t]


def first_sweep(boxes, u_ref, b_ref, d_ref, c_ref, yz_ref, x_ref):
    def one(box, carry):
        tiles = []
        for t in range(TILES):
            cut = slice(128 * t, 128 * (t + 1))
            scale = 0.8 / (6.0 + d_ref[box, :, cut])
            c_ref[box, :, cut] = scale
            tiles.append(scale * b_ref[box, :, cut])
        write_tiles(u_ref, box, tiles)
        put_faces(tiles, yz_ref, x_ref, boxes + box)
        return carry

    lax.fori_loop(0, boxes, one, 0)


def sweep_boxes(boxes, u_ref, b_ref, c_ref, ghosts, out_ref, faces, keep=None):
    yz_from, x_from, nbr_ref = ghosts

    def one(box, carry):
        tiles = tiles_of(u_ref, box)
        sums = beside(tiles, ghosts_of(yz_from, x_from, nbr_ref, box))
        fresh = []
        for t in range(TILES):
            cut = slice(128 * t, 128 * (t + 1))
            fresh.append(
                0.2 * tiles[t] + c_ref[box, :, cut] * (b_ref[box, :, cut] + sums[t])
            )
        if keep is not None:
            kept = keep(box)
            fresh = [t * kept for t in fresh]
        write_tiles(out_ref, box, fresh)
        if faces is not None:
            put_faces(fresh, faces[0], faces[1], boxes + box)
        return carry

    lax.fori_loop(0, boxes, one, 0)


def residual_boxes(boxes, u_ref, b_ref, d_ref, ghosts, r_ref, keep=None):
    yz_from, x_from, nbr_ref = ghosts

    def one(box, carry):
        tiles = tiles_of(u_ref, box)
        sums = beside(tiles, ghosts_of(yz_from, x_from, nbr_ref, box))
        for t in range(TILES):
            cut = slice(128 * t, 128 * (t + 1))
            left = b_ref[box, :, cut] - ((6.0 + d_ref[box, :, cut]) * tiles[t] - sums[t])
            r_ref[pl.ds(pl.multiple_of(box * 32, 32), 32), cut] = (
                left if keep is None else left * keep(box)
            )
        return carry

    lax.fori_loop(0, boxes, one, 0)


def down_kernel(
    n_box,
    n_node,
    fine_b,
    fine_d,
    count_ref,
    fine_nbr,
    cover_ref,
    source_ref,
    coarse_d,
    coarse_nbr,
    place_ref,
    bottom_d,
    fine_u,
    fine_c,
    coarse_u,
    coarse_b,
    coarse_c,
    reach,
    blocks_out,
    places_out,
    u_first,
    yz_fine_0,
    x_fine_0,
    yz_fine_1,
    x_fine_1,
    slab_c,
    rest_ref,
    octants,
    placed,
    lifted,
    found_at,
    cu_first,
    yz_coarse_0,
    x_coarse_0,
    yz_coarse_1,
    x_coarse_1,
    blocks,
    places,
    send_sems,
    recv_sems,
    local_sem,
):
    here = Place(n_box, n_node)
    copies = Copies(send_sems, recv_sems)
    boxes = fine_b.shape[0]
    here.barrier([here.at_box(1), here.at_box(-1), here.at_box(2), here.at_box(-2)])

    rows_x, rows_y = bottom_d.shape[0], bottom_d.shape[1]

    def scale_plane(x, carry):
        slab_c[x] = 0.8 / (6.0 + bottom_d[x])
        return carry

    lax.fori_loop(0, rows_x, scale_plane, 0)
    own_x, own_y = pl.ds(HALO, rows_x), pl.ds(Y_HALO, rows_y)
    own_copy = pltpu.make_async_copy(slab_c, reach.at[own_x, own_y], local_sem)
    own_copy.start()
    halo_y = [
        copies.start(
            slab_c.at[:, pl.ds(rows_y - Y_HALO, Y_HALO)],
            reach.at[own_x, pl.ds(0, Y_HALO)],
            here.at_node(1),
        ),
        copies.start(
            slab_c.at[:, pl.ds(0, Y_HALO)],
            reach.at[own_x, pl.ds(Y_HALO + rows_y, Y_HALO)],
            here.at_node(-1),
        ),
    ]

    first_sweep(boxes, u_first, fine_b, fine_d, fine_c, yz_fine_0, x_fine_0)
    faces = send_faces(copies, here, yz_fine_0, x_fine_0, boxes)

    for target in range(8 * n_node):
        slot = jnp.int32(-1)
        for box in range(boxes):
            slot = jnp.where(cover_ref[0, box] == target, box, slot)
        found_at[target] = slot

    own_copy.wait()
    arrived(halo_y)
    some = HALO - rows_x
    halo_x = [
        copies.start(reach.at[own_x], reach.at[pl.ds(HALO - rows_x, rows_x)], here.at_box(1)),
        copies.start(reach.at[own_x], reach.at[pl.ds(HALO + rows_x, rows_x)], here.at_box(-1)),
        copies.start(
            reach.at[pl.ds(HALO + rows_x - some, some)], reach.at[pl.ds(0, some)], here.at_box(2)
        ),
        copies.start(
            reach.at[pl.ds(HALO, some)],
            reach.at[pl.ds(HALO + 2 * rows_x, some)],
            here.at_box(-2),
        ),
    ]

    arrived(faces)
    sweep_boxes(
        boxes,
        u_first,
        fine_b,
        fine_c,
        (yz_fine_0, x_fine_0, fine_nbr),
        fine_u,
        (yz_fine_1, x_fine_1),
    )
    faces = send_faces(copies, here, yz_fine_1, x_fine_1, boxes)
    fold_yz = one_hot_of(
        (1024, 256), lambda r, l: (r // 64 == l // 16) & (r % 32 // 2 == l % 16)
    )
    fold_x = one_hot_of((16 * boxes, 32 * boxes), lambda r, l: l // 2 == r)
    arrived(faces)
    live = count_ref[0, 0]
    residual_boxes(
        boxes,
        fine_u,
        fine_b,
        fine_d,
        (yz_fine_1, x_fine_1, fine_nbr),
        rest_ref,
        lambda box: jnp.where(box < live, 1.0, 0.0).astype(F32),
    )
    cubes = pick_left(fold_x, pick_right(rest_ref[...], fold_yz)) * 0.5
    for box in range(boxes):
        octants[box] = cubes[16 * box : 16 * (box + 1)]

    def place_one(target, carry):
        slot = found_at[target]
        kept = jnp.where(slot >= 0, 1.0, 0.0).astype(F32)
        placed[target] = octants[jnp.maximum(slot, 0)] * kept
        return carry

    lax.fori_loop(0, 8 * n_node, place_one, 0)
    given = []
    for step, (other, device) in enumerate(here.peers_node()):
        given.append(
            copies.start(
                placed.at[pl.ds(pl.multiple_of(other * 8, 8), 8)], lifted.at[step], device
            )
        )
    spread = one_hot_of(
        (512, 512),
        lambda r, l: (r // 256 == l % 32 // 16) & (r % 256 // 16 == l // 32) & (r % 16 == l % 16),
    )
    arrived(given)
    total = placed[pl.ds(pl.multiple_of(here.node * 8, 8), 8)]
    for step in range(n_node - 1):
        total = total + lifted[step]
    pairs = jnp.concatenate(
        [jnp.concatenate([total[2 * k], total[2 * k + 1]], axis=1) for k in range(4)], axis=0
    )
    grown = pick_right(pairs, spread)
    for k in range(4):
        at_x, at_y = 16 * (k // 2), 512 * (k % 2)
        coarse_b[0, at_x : at_x + 16, at_y : at_y + 512] = (
            source_ref[0, at_x : at_x + 16, at_y : at_y + 512] + grown[16 * k : 16 * (k + 1)]
        )

    first_sweep(1, cu_first, coarse_b, coarse_d, coarse_c, yz_coarse_0, x_coarse_0)
    faces = send_faces(copies, here, yz_coarse_0, x_coarse_0, 1)
    arrived(faces)
    sweep_boxes(
        1,
        cu_first,
        coarse_b,
        coarse_c,
        (yz_coarse_0, x_coarse_0, coarse_nbr),
        coarse_u,
        (yz_coarse_1, x_coarse_1),
    )
    faces = send_faces(copies, here, yz_coarse_1, x_coarse_1, 1)
    fold_quarter = one_hot_of(
        (1024, 128), lambda r, l: (r // 128 == l % 64 // 8) & (r % 32 // 4 == l % 8)
    )
    arrived(faces)
    residual_boxes(
        1,
        coarse_u,
        coarse_b,
        coarse_d,
        (yz_coarse_1, x_coarse_1, coarse_nbr),
        rest_ref,
    )
    folded = pick_right(rest_ref[0:32], fold_quarter)
    early = pick_left(one_hot_of((8, 32), lambda r, l: l // 4 == r), folded)
    late = pick_left(one_hot_of((8, 32), lambda r, l: l // 4 == r + 4), folded)
    block = jnp.where(lanes_of((8, 128)) < 64, early, late) * 0.25
    y, z, core, node = here.y, here.z, here.core, here.node
    blocks[y, z, core, node] = block[0:4]
    places[y, z, core, node] = jnp.full((1, 128), place_ref[0], I32)

    def both(part, device):
        return [copies.start(part(ref), part(ref), device) for ref in (blocks, places)]

    waits = []
    for _, device in here.peers_node():
        waits += both(lambda ref: ref.at[y, z, core, node], device)
    arrived(waits)
    waits = []
    for _, device in here.peers_z():
        waits += both(lambda ref: ref.at[y, z, core], device)
    arrived(waits)
    waits = []
    for _, device in here.peers_y():
        waits += both(lambda ref: ref.at[y, :, core], device)
    arrived(waits)
    arrived(both(lambda ref: ref.at[:, :, core], here.peer_core()[1]))

    blocks_out[...] = blocks[...]
    row = jnp.zeros((1, 128), I32)
    lane = lanes_of((1, 128))
    number = 0
    for at_y in range(here.ny):
        for at_z in range(here.nz):
            for at_core in range(here.nc):
                for at_node in range(n_node):
                    row = jnp.where(lane == number, places[at_y, at_z, at_core, at_node], row)
                    number += 1
    places_out[...] = row

    arrived(halo_x)
    copies.finish()


def bottom_kernel(
    n_box, n_node, rows_x, rows_y, places, reach, blocks, out, scale, source, first, second
):
    deep, wide, long = reach.shape
    count = n_box * n_node
    per_side = long // 8
    at_x = lax.axis_index("box") * rows_x - HALO
    at_y = lax.axis_index("node") * rows_y - Y_HALO
    edge_y = per_side * 8
    tile_z = one_hot_of((128, long), lambda r, l: r % 8 == l % 8)
    untile_z = one_hot_of((long, 128), lambda r, l: r % 8 == l % 8)
    lane, row = lanes_of((8, 128)), rows_of((8, 128))
    block_z = lanes_of((64, long)) // 8

    def clear(x, carry):
        source[x] = jnp.zeros((wide, long), F32)
        return carry

    lax.fori_loop(0, source.shape[0], clear, 0)
    out[...] = jnp.zeros(out.shape, F32)

    def where_is(number):
        place = places[0, number]
        return (
            place // (per_side * per_side) * 8 - at_x,
            place // per_side % per_side * 8 - at_y,
            place % per_side,
        )

    def put(number, carry):
        x, y, z = where_is(number)

        @pl.when((x > -8) & (x < deep) & (y >= 0) & (y < wide))
        def _():
            block = blocks[number]
            parts = []
            for ix in range(8):
                spread = jnp.broadcast_to(block[ix % 4 : ix % 4 + 1], (8, 128))
                parts.append(jnp.where(lane // 8 == row + 8 * (ix // 4), spread, 0.0))
            tiled = pick_right(jnp.concatenate(parts, axis=0), tile_z)
            tiled = jnp.where(block_z == z, tiled, 0.0)
            rows = pl.ds(pl.multiple_of(y, 8), 8)
            for ix in range(8):
                source[x + ix + 8, rows, :] += tiled[8 * ix : 8 * (ix + 1)]

        return carry

    lax.fori_loop(0, count, put, 0)

    plane_y = rows_of((wide, long)) + at_y
    inside_y = (plane_y >= 0) & (plane_y < edge_y)

    def begin(x, carry):
        inside_x = jnp.where((at_x + x >= 0) & (at_x + x < rows_x * n_box), 1.0, 0.0)
        masked = jnp.where(inside_y, reach[x] * inside_x.astype(F32), 0.0)
        scale[x] = masked
        first[x] = masked * source[x + 8]
        return carry

    lax.fori_loop(0, deep, begin, 0)

    refs = (first, second)
    for sweep_no in range(HALO):
        left = HALO - 1 - sweep_no
        margin = (left + 7) // 8 * 8
        tall = rows_y + 2 * margin
        low = Y_HALO - margin
        here, there = refs[sweep_no % 2], refs[(sweep_no + 1) % 2]
        cut = slice(low, low + tall)
        z = lanes_of((tall, long))

        def plane(x, carry):
            mid = here[x, cut, :]
            around = here[x - 1, cut, :] + here[x + 1, cut, :]
            if low > 0:
                around += here[x, low - 1 : low + tall - 1, :]
                around += here[x, low + 1 : low + tall + 1, :]
            else:
                around += pltpu.roll(mid, 1, 0) + pltpu.roll(mid, tall - 1, 0)
            around += jnp.where(z == 0, 0.0, pltpu.roll(mid, 1, 1))
            around += jnp.where(z == long - 1, 0.0, pltpu.roll(mid, long - 1, 1))
            there[x, cut, :] = 0.2 * mid + scale[x, cut, :] * (source[x + 8, cut, :] + around)
            return carry

        lax.fori_loop(HALO - left, HALO + rows_x + left, plane, 0)
    solved = refs[HALO % 2]

    def take(number, carry):
        x, y, z = where_is(number)

        @pl.when((x == HALO) & (y >= Y_HALO) & (y < Y_HALO + rows_y))
        def _():
            rows = pl.ds(pl.multiple_of(y, 8), 8)
            stack = jnp.concatenate([solved[HALO + ix, rows, :] for ix in range(8)], axis=0)
            spread = pick_right(jnp.where(block_z == z, stack, 0.0), untile_z)
            lines = []
            for ix in range(8):
                mine = jnp.where(
                    lane // 8 == row + 8 * (ix // 4), spread[8 * ix : 8 * (ix + 1)], 0.0
                )
                lines.append(jnp.sum(mine, axis=0, keepdims=True))
            for ix in range(4):
                out[number, ix : ix + 1] = lines[ix] + lines[ix + 4]

        return carry

    lax.fori_loop(0, count, take, 0)


def up_kernel(
    n_box,
    n_node,
    parts,
    fine_u,
    fine_c,
    fine_b,
    count_ref,
    fine_nbr,
    cover_ref,
    coarse_u,
    coarse_b,
    coarse_c,
    coarse_nbr,
    fine_out,
    coarse_out,
    from_core,
    sum_core,
    from_y,
    sum_y,
    from_z,
    sum_z,
    from_node,
    own_block,
    cu_first,
    cu_second,
    yz_coarse_0,
    x_coarse_0,
    yz_coarse_1,
    x_coarse_1,
    octants,
    picked,
    u_first,
    u_second,
    yz_fine_0,
    x_fine_0,
    yz_fine_1,
    x_fine_1,
    send_sems,
    recv_sems,
):
    here = Place(n_box, n_node)
    copies = Copies(send_sems, recv_sems)
    boxes = fine_u.shape[0]
    here.barrier([])

    other, device = here.peer_core()
    arrived([copies.start(parts.at[:, :, other], from_core, device)])
    sum_core[...] = parts[:, :, here.core] + from_core[...]
    waits = [
        copies.start(sum_core.at[other], from_y.at[step], device)
        for step, (other, device) in enumerate(here.peers_y())
    ]
    arrived(waits)
    sum_y[...] = sum_core[here.y] + sum([from_y[step] for step in range(here.ny - 1)])
    waits = [
        copies.start(sum_y.at[other], from_z.at[step], device)
        for step, (other, device) in enumerate(here.peers_z())
    ]
    arrived(waits)
    sum_z[...] = sum_y[here.z] + sum([from_z[step] for step in range(here.nz - 1)])
    waits = [
        copies.start(sum_z.at[other], from_node.at[step], device)
        for step, (other, device) in enumerate(here.peers_node())
    ]
    grow_quarter = one_hot_of(
        (128, 1024), lambda r, l: r == l // 128 * 8 + l % 32 // 4
    )
    arrived(waits)
    block = sum_z[here.node] + sum([from_node[step] for step in range(n_node - 1)])
    own_block[0:4] = block
    own_block[4:8] = pltpu.roll(block, 64, 1)
    grown = pick_right(own_block[...], grow_quarter)
    grown = pick_left(one_hot_of((32, 8), lambda r, l: r // 4 == l), grown)
    cu_first[0] = coarse_u[0] + grown
    put_faces(tiles_of(cu_first, 0), yz_coarse_0, x_coarse_0, 1)
    faces = send_faces(copies, here, yz_coarse_0, x_coarse_0, 1)
    arrived(faces)
    sweep_boxes(
        1,
        cu_first,
        coarse_b,
        coarse_c,
        (yz_coarse_0, x_coarse_0, coarse_nbr),
        cu_second,
        (yz_coarse_1, x_coarse_1),
    )
    faces = send_faces(copies, here, yz_coarse_1, x_coarse_1, 1)
    split = one_hot_of(
        (512, 512),
        lambda r, l: (l // 256 == r % 32 // 16) & (l % 256 // 16 == r // 32) & (l % 16 == r % 16),
    )
    arrived(faces)
    sweep_boxes(
        1,
        cu_second,
        coarse_b,
        coarse_c,
        (yz_coarse_1, x_coarse_1, coarse_nbr),
        coarse_out,
        None,
    )

    quarters = jnp.concatenate(
        [
            coarse_out[0, 16 * (k // 2) : 16 * (k // 2) + 16, 512 * (k % 2) : 512 * (k % 2) + 512]
            for k in range(4)
        ],
        axis=0,
    )
    cubes = pick_right(quarters, split)
    base = pl.multiple_of(here.node * 8, 8)
    for k in range(8):
        octants[base + k] = cubes[16 * (k // 2) : 16 * (k // 2) + 16, 256 * (k % 2) : 256 * (k % 2) + 256]
    own = octants.at[pl.ds(base, 8)]
    waits = [copies.start(own, own, device) for _, device in here.peers_node()]
    grow_yz = one_hot_of(
        (256, 1024), lambda r, l: (l // 64 == r // 16) & (l % 32 // 2 == r % 16)
    )
    grow_x = one_hot_of((32 * boxes, 16 * boxes), lambda r, l: r // 2 == l)
    arrived(waits)
    for box in range(boxes):
        picked[16 * box : 16 * (box + 1)] = octants[cover_ref[0, box]]
    tall = pick_right(pick_left(grow_x, picked[...]), grow_yz)
    for box in range(boxes):
        u_first[box] = fine_u[box] + tall[32 * box : 32 * (box + 1)]

    def faces_of(box, carry):
        put_faces(tiles_of(u_first, box), yz_fine_0, x_fine_0, boxes + box)
        return carry

    lax.fori_loop(0, boxes, faces_of, 0)
    arrived(send_faces(copies, here, yz_fine_0, x_fine_0, boxes))
    sweep_boxes(
        boxes,
        u_first,
        fine_b,
        fine_c,
        (yz_fine_0, x_fine_0, fine_nbr),
        u_second,
        (yz_fine_1, x_fine_1),
    )
    arrived(send_faces(copies, here, yz_fine_1, x_fine_1, boxes))
    live = count_ref[0, 0]
    sweep_boxes(
        boxes,
        u_second,
        fine_b,
        fine_c,
        (yz_fine_1, x_fine_1, fine_nbr),
        fine_out,
        None,
        lambda box: jnp.where(box < live, 1.0, 0.0).astype(F32),
    )
    copies.finish()


VMEM, SMEM, ANY = (
    pl.BlockSpec(memory_space=pltpu.VMEM),
    pl.BlockSpec(memory_space=pltpu.SMEM),
    pl.BlockSpec(memory_space=pl.ANY),
)


def shards(
    n_box,
    n_node,
    fine_rhs,
    fine_diag,
    fine_count,
    fine_nbr,
    fine_cover,
    coarse_source,
    coarse_diag,
    coarse_nbr,
    coarse_place,
    bottom_diag,
):
    boxes = fine_rhs.shape[0]
    ny, nz, nc = grid_of(n_box)
    rows_x, rows_y, long = bottom_diag.shape
    deep, wide = rows_x + 2 * HALO, rows_y + 2 * Y_HALO
    count = n_box * n_node

    def like(shape, kind=F32):
        return jax.ShapeDtypeStruct(shape, kind)

    fine, coarse = (boxes, 32, 1024), (1, 32, 1024)
    grid = (ny, nz, nc, n_node)
    limit = 48 * 1024 * 1024
    fine_u, fine_c, coarse_u, coarse_b, coarse_c, reach, blocks, places = pl.pallas_call(
        functools.partial(down_kernel, n_box, n_node),
        out_shape=(
            like(fine),
            like(fine),
            like(coarse),
            like(coarse),
            like(coarse),
            like((deep, wide, long)),
            like(grid + (4, 128)),
            like((1, 128), I32),
        ),
        in_specs=[VMEM, VMEM, SMEM, SMEM, SMEM, VMEM, VMEM, SMEM, SMEM, VMEM],
        out_specs=(VMEM, VMEM, VMEM, VMEM, VMEM, ANY, VMEM, VMEM),
        scratch_shapes=[
            pltpu.VMEM(fine, F32),
            pltpu.VMEM((3 * boxes, 32, 128), F32),
            pltpu.VMEM((3 * boxes, 2, 1024), F32),
            pltpu.VMEM((3 * boxes, 32, 128), F32),
            pltpu.VMEM((3 * boxes, 2, 1024), F32),
            pltpu.VMEM((rows_x, rows_y, long), F32),
            pltpu.VMEM((32 * boxes, 1024), F32),
            pltpu.VMEM((boxes, 16, 256), F32),
            pltpu.VMEM((8 * n_node, 16, 256), F32),
            pltpu.VMEM((n_node - 1, 8, 16, 256), F32),
            pltpu.SMEM((8 * n_node,), I32),
            pltpu.VMEM(coarse, F32),
            pltpu.VMEM((3, 32, 128), F32),
            pltpu.VMEM((3, 2, 1024), F32),
            pltpu.VMEM((3, 32, 128), F32),
            pltpu.VMEM((3, 2, 1024), F32),
            pltpu.VMEM(grid + (4, 128), F32),
            pltpu.VMEM(grid + (1, 128), I32),
            pltpu.SemaphoreType.DMA((64,)),
            pltpu.SemaphoreType.DMA((64,)),
            pltpu.SemaphoreType.DMA,
        ],
        compiler_params=pltpu.CompilerParams(
            collective_id=0, has_side_effects=True, vmem_limit_bytes=limit
        ),
        name="down",
    )(
        fine_rhs,
        fine_diag,
        fine_count,
        fine_nbr,
        fine_cover,
        coarse_source,
        coarse_diag,
        coarse_nbr,
        coarse_place,
        bottom_diag,
    )
    parts = pl.pallas_call(
        functools.partial(bottom_kernel, n_box, n_node, rows_x, rows_y),
        out_shape=like((count, 4, 128)),
        in_specs=[SMEM, VMEM, VMEM],
        out_specs=VMEM,
        scratch_shapes=[
            pltpu.VMEM((deep, wide, long), F32),
            pltpu.VMEM((deep + 16, wide, long), F32),
            pltpu.VMEM((deep, wide, long), F32),
            pltpu.VMEM((deep, wide, long), F32),
        ],
        compiler_params=pltpu.CompilerParams(vmem_limit_bytes=limit),
        name="bottom",
    )(places, reach, blocks.reshape(count, 4, 128))
    fine_out, coarse_out = pl.pallas_call(
        functools.partial(up_kernel, n_box, n_node),
        out_shape=(like(fine), like(coarse)),
        in_specs=[VMEM, VMEM, VMEM, VMEM, SMEM, SMEM, SMEM, VMEM, VMEM, VMEM, SMEM],
        out_specs=(VMEM, VMEM),
        scratch_shapes=[
            pltpu.VMEM((ny, nz, n_node, 4, 128), F32),
            pltpu.VMEM((ny, nz, n_node, 4, 128), F32),
            pltpu.VMEM((ny - 1, nz, n_node, 4, 128), F32),
            pltpu.VMEM((nz, n_node, 4, 128), F32),
            pltpu.VMEM((nz - 1, n_node, 4, 128), F32),
            pltpu.VMEM((n_node, 4, 128), F32),
            pltpu.VMEM((n_node - 1, 4, 128), F32),
            pltpu.VMEM((8, 128), F32),
            pltpu.VMEM(coarse, F32),
            pltpu.VMEM(coarse, F32),
            pltpu.VMEM((3, 32, 128), F32),
            pltpu.VMEM((3, 2, 1024), F32),
            pltpu.VMEM((3, 32, 128), F32),
            pltpu.VMEM((3, 2, 1024), F32),
            pltpu.VMEM((8 * n_node, 16, 256), F32),
            pltpu.VMEM((16 * boxes, 256), F32),
            pltpu.VMEM(fine, F32),
            pltpu.VMEM(fine, F32),
            pltpu.VMEM((3 * boxes, 32, 128), F32),
            pltpu.VMEM((3 * boxes, 2, 1024), F32),
            pltpu.VMEM((3 * boxes, 32, 128), F32),
            pltpu.VMEM((3 * boxes, 2, 1024), F32),
            pltpu.SemaphoreType.DMA((48,)),
            pltpu.SemaphoreType.DMA((48,)),
        ],
        compiler_params=pltpu.CompilerParams(
            collective_id=1, has_side_effects=True, vmem_limit_bytes=limit
        ),
        name="up",
    )(
        parts.reshape(grid + (4, 128)),
        fine_u,
        fine_c,
        fine_rhs,
        fine_count,
        fine_nbr,
        fine_cover,
        coarse_u,
        coarse_b,
        coarse_c,
        coarse_nbr,
    )
    return fine_out, coarse_out


def solution(mesh):
    n_box, n_node = mesh.shape["box"], mesh.shape["node"]
    return jax.shard_map(
        functools.partial(shards, n_box, n_node),
        mesh=mesh,
        in_specs=(
            P(("box", "node"), None, None),
            P(("box", "node"), None, None),
            P("box", "node"),
            P(("box", "node"), None),
            P("box", "node"),
            P(("box", "node"), None, None),
            P(("box", "node"), None, None),
            P(("box", "node"), None),
            P(("box", "node")),
            P("box", "node", None),
        ),
        out_specs=(P(("box", "node"), None, None), P(("box", "node"), None, None)),
        check_vma=False,
    )
```

time: 992 us -> 168 us (0.17); the launches traced: 973 us -> 167 us
  waiting for transfers between devices: 290 us -> 0 us
  local copies, waits for them, and re-layouts: 298 us -> 10.8 us
  Pallas kernels: 0 us -> 155 us
  blocking collectives: 145 us -> 0 us
  starting transfers between devices: 133 us -> 0 us
  other arithmetic: 88.5 us -> 0 us
  between operations: 17.1 us -> 2.01 us
    psum x1 -> x0, waiting for transfers between devices: 167 us -> none  [shards(): summed = lax.psum(picked, ('box', 'node'))]
    pallas_call x0 -> x3, Pallas kernels: none -> 155 us  [the longest x1 60.4 us: shards(): pl.pallas_call(functools.partial(down_kernel, n_box, n_node), out_shape=(...]
    ppermute x60 -> x0, starting transfers between devices: 133 us -> none  [the longest x30 94.5 us: padded_2(): before = lax.ppermute(last, axis, up)]
    reshape x18 -> x0, local copies, waits for them, and re-layouts: 102 us -> none  [the longest x4 18.3 us: shift_sum(): jnp.repeat(high_z, edge_len, axis=2)]
    ppermute x60 -> x0, waiting for transfers between devices: 99.5 us -> none  [the longest x30 99.4 us: padded_2(): after = lax.ppermute(leading, axis, down)]
    all_gather x2 -> x0, blocking collectives: 76.2 us -> none  [the longest x1 62.9 us: shards(): lax.all_gather(blocks, ('box', 'node'), axis=0, tiled=True)]
    unnamed x1 -> x0, blocking collectives: 69.1 us -> none
    slice x117 -> x0, local copies, waits for them, and re-layouts: 50.8 us -> none  [the longest x22 7.82 us: padded_2(): leading = lax.slice_in_dim(shard, 0, width, axis=dim)]
  transfers between devices with their start and end apart: 62 -> 0, of which waited for: 31 -> 0; matrix products, arithmetic and copies ran while one was open for 3% -> 0% of each run, Pallas kernels for 0% -> 0%
where the time goes in v1:
time: 168 us; the launch traced here: 167 us
  Pallas kernels  155 us (92%)
  local copies, waits for them, and re-layouts  10.8 us (6%)
  between operations  2.01 us (1%)
    pallas_call x1, Pallas kernels, shards(): pl.pallas_call(functools.partial(down_kernel, n_box, n_node), out_shape=(...  60.4 us
    pallas_call x1, Pallas kernels, shards(): pl.pallas_call(functools.partial(up_kernel, n_box, n_node), out_shape=(li...  60 us
    pallas_call x1, Pallas kernels, shards(): pl.pallas_call(functools.partial(bottom_kernel, n_box, n_node, rows_x, ro...  34.3 us
    unnamed x28, local copies, waits for them, and re-layouts  10.8 us

profile of v1, /device:TPU:0, one launch (start us, length us, event | category | flops | bytes accessed | tf_op | source)
XLA Modules:
  0.0 167.5 jit_solution(546557704286789614)
XLA Ops:
  1.9 0.0 copy-start
  1.9 1.2 copy-done
  3.2 0.0 copy-start.3
  3.2 1.2 copy-done.3
  4.4 0.0 copy-start.4
  4.4 1.0 copy-done.4
  5.4 0.0 copy-start.5
  5.4 0.9 copy-done.5
  6.3 0.0 copy-start.6
  6.3 0.9 copy-done.6
  7.2 0.0 copy-start.7
  7.2 0.7 copy-done.7
  7.9 0.0 copy-start.9
  7.9 0.7 copy-done.9
  8.6 0.0 copy-start.11
  8.6 0.7 copy-done.11
  9.2 0.0 copy-start.1
  9.2 0.0 copy-start.8
  9.2 0.0 copy-start.10
  9.2 0.0 copy-start.12
  9.2 60.4 %down.1 = (f32[8,32,1024]{2,1,0:T(8,128)S(1)}, f32[8,32,1024]{2,1,0:T(8,128)S(1)}, f32[1,32,1024]{2,1,0:T(8,128)S(1)}, f32[1,32,1024]{2,1,0:T(8,128)S(1)}, f32[1...) custom-call(f32[8,32,1024]{2,1,0:T(8,128)S(1)} %copy-done, ...), custom_call_target="tpu_custom_call" | custom-call | tf_op jit(solution)/shard_map/down/pallas_call | solution.py:820
  69.7 0.0 copy-start.2
  69.7 1.8 %copy-done.2 = f32[30,96,256]{2,1,0:T(8,128)S(1)} copy-done((f32[30,96,256]{2,1,0:T(8,128)S(1)}, f32[30,96,256]{2,1,0:T(8,128)}, u32[]{:S(2)}) %copy-start.2) | copy-done | bytes 2949144
  71.5 34.3 %bottom.1 = f32[128,4,128]{2,1,0:T(4,128)S(1)} custom-call(s32[1,128]{1,0:T(1,128)S(1)} %get-tuple-element.10.places, f32[30,96,256]{2,1,0:T(8,128)S(1)} %copy-done.2, f32[128,4,128]{2,1,0:T(4,128)S(1)} %bitcast.3), custom_call_target="tpu_custom_call" | custom-call | tf_op jit(solution)/shard_map/bottom/pallas_call | solution.py:873
  105.9 0.0 copy-done.1
  105.9 0.0 copy-done.8
  105.9 0.0 copy-done.10
  105.9 0.0 copy-done.12
  105.9 60.0 %up.1 = (f32[8,32,1024]{2,1,0:T(8,128)S(1)}, f32[1,32,1024]{2,1,0:T(8,128)S(1)}) custom-call(f32[4,4,2,4,4,128]{5,4,3,2,1,0:T(4,128)S(1)} %bitcast.2, f32[8,32,1024]{2,1,0:T(8,128)S(1)} %get-tuple-element.13.fine_u, f32[8,32,1024]{2,1,0:T(8,128)S(1)} %get-tuple-element.14.fine_c, f32[8,32,1024]{2,1,0:T(8,128)S(1)} %copy-done.1, s32[1,1]{1,0:T(1,128)S(6)} %copy.14.count_ref, ...), custom_call_target="tpu_custom_call" | custom-call | tf_op jit(solution)/shard_map/up/pallas_call | solution.py:887
  165.9 1.0 copy.16
  166.8 0.7 copy.17
Async XLA Ops:
  1.9 1.2 copy-start
  3.2 1.2 copy-start.3
  4.4 1.0 copy-start.4
  5.4 0.9 copy-start.5
  6.3 0.9 copy-start.6
  7.2 0.7 copy-start.7
  7.9 0.7 copy-start.9
  8.6 0.7 copy-start.11
  9.2 96.6 %copy-start.1 = (f32[8,32,1024]{2,1,0:T(8,128)S(1)}, f32[8,32,1024]{2,1,0:T(8,128)}, u32[]{:S(2)}) copy-start(f32[8,32,1024]{2,1,0:T(8,128)} %fine_b.3) | copy-start | bytes 3145732
  9.2 96.6 %copy-start.8 = (s32[8,6]{1,0:T(8,128)S(1)}, s32[8,6]{1,0:T(8,128)}, u32[]{:S(2)}) copy-start(s32[8,6]{1,0:T(8,128)} %fine_nbr.3) | copy-start | bytes 580
  9.2 96.6 %copy-start.10 = (s32[1,8]{1,0:T(1,128)S(1)}, s32[1,8]{1,0:T(1,128)}, u32[]{:S(2)}) copy-start(s32[1,8]{1,0:T(1,128)} %cover_ref.3) | copy-start | bytes 100
  9.2 96.7 %copy-start.12 = (s32[1,6]{1,0:T(1,128)S(1)}, s32[1,6]{1,0:T(1,128)}, u32[]{:S(2)}) copy-start(s32[1,6]{1,0:T(1,128)} %coarse_nbr.3) | copy-start | bytes 76
  69.7 1.8 %copy-start.2 = (f32[30,96,256]{2,1,0:T(8,128)S(1)}, f32[30,96,256]{2,1,0:T(8,128)}, u32[]{:S(2)}) copy-start(f32[30,96,256]{2,1,0:T(8,128)} %get-tuple-element.11.reach) | copy-start | bytes 8847364

commit v2 on v1

v2 whole, which is shorter than its diff:
```python
import functools

import jax
import jax.numpy as jnp
from jax import lax
from jax.experimental import pallas as pl
from jax.experimental.pallas import tpu as pltpu
from jax.sharding import PartitionSpec as P

F32, BF16, I32 = jnp.float32, jnp.bfloat16, jnp.int32
MESH = pl.DeviceIdType.MESH
BOT_ITERS = 12
HALO = BOT_ITERS - 1
Y_HALO = 16
TILES = 8


def grid_of(n_box):
    return {32: (4, 4, 2), 8: (2, 2, 2)}[n_box]


def lanes_of(shape):
    return lax.broadcasted_iota(I32, shape, len(shape) - 1)


def rows_of(shape):
    return lax.broadcasted_iota(I32, shape, len(shape) - 2)


def thirds(a):
    high = a.astype(BF16)
    rest = a - high.astype(F32)
    middle = rest.astype(BF16)
    low = (rest - middle.astype(F32)).astype(BF16)
    return high, middle, low


def pick_right(a, one_hot):
    high, middle, low = [jnp.dot(t, one_hot, preferred_element_type=F32) for t in thirds(a)]
    return high + (middle + low)


def pick_left(one_hot, a):
    high, middle, low = [jnp.dot(one_hot, t, preferred_element_type=F32) for t in thirds(a)]
    return high + (middle + low)


def one_hot_of(shape, test):
    return jnp.where(test(rows_of(shape), lanes_of(shape)), 1.0, 0.0).astype(BF16)


def roll_lanes(a, shift):
    shift = shift % 128
    return a if shift == 0 else pltpu.roll(a, shift, 1)


def tiles_of(ref, box):
    return [ref[box, :, 128 * t : 128 * (t + 1)] for t in range(TILES)]


def pack_faces(tiles):
    lane = lanes_of((32, 128))
    within, quarter = lane & 31, lane >> 5
    first, last = tiles[0], tiles[-1]
    packed = jnp.where(
        quarter == 0,
        first,
        jnp.where(
            quarter == 1,
            jnp.where(within < 16, roll_lanes(first, 40), roll_lanes(first, 24)),
            jnp.where(
                quarter == 2,
                jnp.where(within < 16, roll_lanes(last, -24), roll_lanes(last, -40)),
                last,
            ),
        ),
    )
    for t in range(TILES):
        packed = jnp.where(within == t, roll_lanes(tiles[t], t), packed)
        packed = jnp.where(within == 31 - t, roll_lanes(tiles[t], -t), packed)
    return packed


def put_faces(tiles, yz_ref, x_ref, slot):
    yz_ref[slot] = pack_faces(tiles)
    for t in range(TILES):
        x_ref[slot, 0:1, 128 * t : 128 * (t + 1)] = tiles[t][0:1, :]
        x_ref[slot, 1:2, 128 * t : 128 * (t + 1)] = tiles[t][31:32, :]


def ghosts_of(yz_ref, x_ref, nbr_ref, box):
    def chosen(ref, face):
        which = nbr_ref[box, face]
        kept = jnp.where(which >= 0, 1.0, 0.0).astype(F32)
        return ref[jnp.maximum(which, 0)], kept

    def tile(face):
        value, kept = chosen(yz_ref, face)
        return value * kept

    x_low, low_kept = chosen(x_ref, 0)
    x_high, high_kept = chosen(x_ref, 1)
    return (
        x_low[1:2] * low_kept,
        x_high[0:1] * high_kept,
        tile(2),
        tile(3),
        tile(4),
        tile(5),
    )


def beside(tiles, ghosts):
    x_low, x_high, y_low, y_high, z_low, z_high = ghosts
    lane, row = lanes_of((32, 128)), rows_of((32, 128))
    within = lane & 31
    below = jnp.where(
        within < 8,
        roll_lanes(y_low, 56),
        jnp.where(within < 24, roll_lanes(y_low, 32), roll_lanes(y_low, 72)),
    )
    above = jnp.where(
        within < 8,
        roll_lanes(y_high, 56),
        jnp.where(within < 24, roll_lanes(y_high, 96), roll_lanes(y_high, 72)),
    )
    ups = [below] + [roll_lanes(t, 32) for t in tiles]
    downs = [roll_lanes(t, 96) for t in tiles] + [above]
    sums = []
    for t in range(TILES):
        cut = slice(128 * t, 128 * (t + 1))
        along_x = jnp.where(row == 0, x_low[:, cut], pltpu.roll(tiles[t], 1, 0)) + jnp.where(
            row == 31, x_high[:, cut], pltpu.roll(tiles[t], 31, 0)
        )
        along_y = jnp.where(lane < 32, ups[t], ups[t + 1]) + jnp.where(
            lane >= 96, downs[t + 1], downs[t]
        )
        along_z = jnp.where(
            within == 0, roll_lanes(z_low, t - 31), roll_lanes(tiles[t], 1)
        ) + jnp.where(within == 31, roll_lanes(z_high, 31 - t), roll_lanes(tiles[t], 127))
        sums.append(along_x + along_y + along_z)
    return sums


class Copies:
    def __init__(self, send_sems, recv_sems):
        self.send_sems, self.recv_sems, self.made = send_sems, recv_sems, []

    def start(self, source, target, device):
        number = len(self.made)
        copy = pltpu.make_async_remote_copy(
            src_ref=source,
            dst_ref=target,
            send_sem=self.send_sems.at[number],
            recv_sem=self.recv_sems.at[number],
            device_id=device,
            device_id_type=MESH,
        )
        copy.start()
        self.made.append(copy)
        return copy

    def finish(self):
        for copy in self.made:
            copy.wait_send()


def arrived(copies):
    for copy in copies:
        copy.wait_recv()


class Place:
    def __init__(self, n_box, n_node):
        self.n_box, self.n_node = n_box, n_node
        self.ny, self.nz, self.nc = grid_of(n_box)
        self.box, self.node = lax.axis_index("box"), lax.axis_index("node")
        self.chips = self.ny * self.nz * n_node
        self.core = self.box & 1
        self.z = (self.box >> 1) & (self.nz - 1)
        self.y = (self.box >> 1) >> (self.nz.bit_length() - 1)

    def along_line(self, step):
        total = self.n_box * self.n_node
        other = (self.box * self.n_node + self.node + step + total) % total
        return (other // self.n_node, other % self.n_node)

    def next_node(self, step):
        return (self.node + step + self.n_node) % self.n_node

    def at_node(self, step):
        return (self.box, self.next_node(step))

    def at_box(self, step):
        return ((self.box + step + self.n_box) % self.n_box, self.node)

    def mate(self):
        return (self.box ^ 1, self.node)

    def at_chip(self, step):
        x_bits = self.n_node.bit_length() - 1
        z_bits = self.nz.bit_length() - 1
        x = (self.node + step) & (self.n_node - 1)
        z = (self.z + (step >> x_bits)) & (self.nz - 1)
        y = (self.y + (step >> x_bits + z_bits)) & (self.ny - 1)
        return ((y * self.nz + z) * self.nc + self.core, x)

    def before_chip(self, step):
        x_bits = self.n_node.bit_length() - 1
        z_bits = self.nz.bit_length() - 1
        x = (self.node - (step & self.n_node - 1)) & (self.n_node - 1)
        z = (self.z - (step >> x_bits & self.nz - 1)) & (self.nz - 1)
        y = (self.y - (step >> x_bits + z_bits)) & (self.ny - 1)
        return ((y * self.nz + z) * self.nc + self.core, x)

    def peers_node(self):
        for step in range(1, self.n_node):
            yield self.next_node(step), self.at_node(step)

    def greet(self, more):
        peers = [self.along_line(1), self.along_line(-1)] + more
        peers += [device for _, device in self.peers_node()]
        peers.append(self.mate())
        barrier = pltpu.get_barrier_semaphore()
        for device in peers:
            pl.semaphore_signal(barrier, inc=1, device_id=device, device_id_type=MESH)

        def chip(step, carry):
            pl.semaphore_signal(
                barrier, inc=1, device_id=self.at_chip(step), device_id_type=MESH
            )
            return carry

        lax.fori_loop(1, self.chips, chip, 0)
        self.peer_count = len(peers) + self.chips - 1

    def greeted(self):
        pl.semaphore_wait(pltpu.get_barrier_semaphore(), self.peer_count)


class Swap:
    def __init__(self, here, yz_ref, x_ref, boxes, step, send_sems, recv_sems):
        self.here, self.refs, self.boxes, self.step = here, (yz_ref, x_ref), boxes, step
        self.send_sems, self.recv_sems = send_sems, recv_sems

    def copies(self, chunk):
        made = []
        for number in range(4):
            ref, later = self.refs[number // 2], 2 * (number % 2)
            at = chunk * self.step
            made.append(
                pltpu.make_async_remote_copy(
                    src_ref=ref.at[pl.ds(self.boxes + at, self.step)],
                    dst_ref=ref.at[pl.ds(later * self.boxes + at, self.step)],
                    send_sem=self.send_sems.at[chunk, number],
                    recv_sem=self.recv_sems.at[chunk, number],
                    device_id=self.here.along_line(1 - later),
                    device_id_type=MESH,
                )
            )
        return made

    def start(self, chunk):
        for copy in self.copies(chunk):
            copy.start()

    def arrived(self):
        for chunk in range(self.boxes // self.step):
            for copy in self.copies(chunk):
                copy.wait_recv()

    def finish(self):
        for chunk in range(self.boxes // self.step):
            for copy in self.copies(chunk):
                copy.wait_send()


def by_chunks(boxes, swap, one):
    step = min(boxes, 2)

    def some(chunk, carry):
        for number in range(step):
            one(chunk * step + number, 0)
        if swap is not None:
            swap.start(chunk)
        return carry

    lax.fori_loop(0, boxes // step, some, 0)


class Spread:
    def __init__(self, here, source, target, device, send_sems, recv_sems):
        self.here, self.source, self.target, self.device = here, source, target, device
        self.send_sems, self.recv_sems = send_sems, recv_sems

    def copy(self, step):
        return pltpu.make_async_remote_copy(
            src_ref=self.source(step),
            dst_ref=self.target(step),
            send_sem=self.send_sems.at[step],
            recv_sem=self.recv_sems.at[step],
            device_id=self.device(step),
            device_id_type=MESH,
        )

    def each(self, act):
        def one(step, carry):
            act(self.copy(step))
            return carry

        lax.fori_loop(1, self.here.chips, one, 0)

    def start(self):
        self.each(lambda copy: copy.start())

    def arrived(self):
        self.each(lambda copy: copy.wait_recv())

    def finish(self):
        self.each(lambda copy: copy.wait_send())


def write_tiles(ref, box, tiles):
    for t in range(TILES):
        ref[box, :, 128 * t : 128 * (t + 1)] = tiles[t]


def first_sweep(boxes, u_ref, b_ref, d_ref, c_ref, swap, ready=None):
    def one(box, carry):
        if ready is not None:
            ready(box)
        scales, tiles = [], []
        for t in range(TILES):
            cut = slice(128 * t, 128 * (t + 1))
            scales.append(0.8 / (6.0 + d_ref[box, :, cut]))
            tiles.append(scales[t] * b_ref[box, :, cut])
        write_tiles(c_ref, box, scales)
        write_tiles(u_ref, box, tiles)
        put_faces(tiles, *swap.refs, boxes + box)

    by_chunks(boxes, swap, one)


def sweep_boxes(boxes, u_ref, b_ref, c_ref, came, nbr_ref, out_ref, swap, keep=None):
    yz_from, x_from = came.refs

    def one(box, carry):
        tiles = tiles_of(u_ref, box)
        sums = beside(tiles, ghosts_of(yz_from, x_from, nbr_ref, box))
        fresh = []
        for t in range(TILES):
            cut = slice(128 * t, 128 * (t + 1))
            fresh.append(
                0.2 * tiles[t] + c_ref[box, :, cut] * (b_ref[box, :, cut] + sums[t])
            )
        if keep is not None:
            kept = keep(box)
            fresh = [t * kept for t in fresh]
        write_tiles(out_ref, box, fresh)
        if swap is not None:
            put_faces(fresh, *swap.refs, boxes + box)

    by_chunks(boxes, swap, one)


def residual_boxes(boxes, u_ref, b_ref, d_ref, came, nbr_ref, r_ref, keep=None):
    yz_from, x_from = came.refs

    def one(box, carry):
        tiles = tiles_of(u_ref, box)
        sums = beside(tiles, ghosts_of(yz_from, x_from, nbr_ref, box))
        rests = []
        for t in range(TILES):
            cut = slice(128 * t, 128 * (t + 1))
            left = b_ref[box, :, cut] - ((6.0 + d_ref[box, :, cut]) * tiles[t] - sums[t])
            rests.append(left if keep is None else left * keep(box))
        for t in range(TILES):
            r_ref[pl.ds(pl.multiple_of(box * 32, 32), 32), 128 * t : 128 * (t + 1)] = rests[t]

    by_chunks(boxes, None, one)


def down_kernel(
    n_box,
    n_node,
    fine_b_in,
    fine_d_in,
    count_ref,
    fine_nbr,
    cover_ref,
    source_in,
    coarse_d_in,
    coarse_nbr,
    place_ref,
    bottom_d_in,
    fine_u,
    fine_c,
    coarse_u,
    coarse_b,
    coarse_c,
    reach,
    blocks_out,
    places_out,
    fine_b,
    fine_d,
    source_ref,
    coarse_d,
    bottom_d,
    u_first,
    yz_fine_0,
    x_fine_0,
    yz_fine_1,
    x_fine_1,
    slab_c,
    rest_ref,
    octants,
    placed,
    lifted,
    found_at,
    cu_first,
    yz_coarse_0,
    x_coarse_0,
    yz_coarse_1,
    x_coarse_1,
    blocks,
    places,
    send_sems,
    recv_sems,
    local_sem,
    fine_sems,
    input_sems,
    fine_sent,
    fine_came,
    coarse_sent,
    coarse_came,
    spread_sent,
    spread_came,
):
    here = Place(n_box, n_node)
    copies = Copies(send_sems, recv_sems)
    boxes = fine_b.shape[0]

    def fine_input(box, number):
        pair = ((fine_b_in, fine_b), (fine_d_in, fine_d))[number]
        return pltpu.make_async_copy(pair[0].at[box], pair[1].at[box], fine_sems.at[number, box])

    for box in range(boxes):
        fine_input(box, 0).start()
        fine_input(box, 1).start()
    inputs = [
        pltpu.make_async_copy(source, target, input_sems.at[number])
        for number, (source, target) in enumerate(
            ((bottom_d_in, bottom_d), (source_in, source_ref), (coarse_d_in, coarse_d))
        )
    ]
    for copy in inputs:
        copy.start()
    here.greet([here.at_box(1), here.at_box(-1), here.at_box(2), here.at_box(-2)])

    def ready(box):
        fine_input(box, 0).wait()
        fine_input(box, 1).wait()

    core = here.core
    places[core, 0] = jnp.full((1, 128), place_ref[0], I32)
    fine_swaps = [
        Swap(here, yz, x, boxes, 2, fine_sent.at[number], fine_came.at[number])
        for number, (yz, x) in enumerate(((yz_fine_0, x_fine_0), (yz_fine_1, x_fine_1)))
    ]
    coarse_swaps = [
        Swap(here, yz, x, 1, 1, coarse_sent.at[number], coarse_came.at[number])
        for number, (yz, x) in enumerate(((yz_coarse_0, x_coarse_0), (yz_coarse_1, x_coarse_1)))
    ]
    spreads = [
        Spread(
            here,
            lambda step, ref=ref: ref.at[core, 0],
            lambda step, ref=ref: ref.at[core, step],
            here.at_chip,
            spread_sent.at[number],
            spread_came.at[number],
        )
        for number, ref in enumerate((places, blocks))
    ]

    here.greeted()
    first_sweep(boxes, u_first, fine_b, fine_d, fine_c, fine_swaps[0], ready)

    rows_x, rows_y = bottom_d.shape[0], bottom_d.shape[1]
    inputs[0].wait()

    part_z = one_hot_of((256, 256), lambda r, l: r == ((l & 127) << 1) + (l >> 7))

    def scale_plane(x, carry):
        slab_c[x] = pick_right(0.8 / (6.0 + bottom_d[x]), part_z)
        return carry

    lax.fori_loop(0, rows_x, scale_plane, 0)
    own_x, own_y = pl.ds(HALO, rows_x), pl.ds(Y_HALO, rows_y)
    own_copy = pltpu.make_async_copy(slab_c, reach.at[own_x, own_y], local_sem)
    own_copy.start()
    sides_y = (pl.ds(0, Y_HALO), pl.ds(Y_HALO + rows_y, Y_HALO))
    halo_y = [
        copies.start(
            slab_c.at[:, pl.ds(rows_y - Y_HALO, Y_HALO)],
            reach.at[own_x, sides_y[0]],
            here.at_node(1),
        ),
        copies.start(
            slab_c.at[:, pl.ds(0, Y_HALO)],
            reach.at[own_x, sides_y[1]],
            here.at_node(-1),
        ),
    ]
    some = HALO - rows_x
    to_x = (
        (1, 0, rows_x, HALO - rows_x),
        (-1, 0, rows_x, HALO + rows_x),
        (2, rows_x - some, some, 0),
        (-2, 0, some, HALO + 2 * rows_x),
    )
    halo_x = [
        copies.start(
            slab_c.at[pl.ds(first, wide)],
            reach.at[pl.ds(target, wide), own_y],
            here.at_box(step),
        )
        for step, first, wide, target in to_x
    ]
    spreads[0].start()

    for target in range(8 * n_node):
        slot = jnp.int32(-1)
        for box in range(boxes):
            slot = jnp.where(cover_ref[0, box] == target, box, slot)
        found_at[target] = slot

    own_copy.wait()
    arrived(halo_y)
    for step, first, wide, target in to_x:
        for side in sides_y:
            halo_x.append(
                copies.start(
                    reach.at[pl.ds(HALO + first, wide), side],
                    reach.at[pl.ds(target, wide), side],
                    here.at_box(step),
                )
            )

    fine_swaps[0].arrived()
    sweep_boxes(
        boxes, u_first, fine_b, fine_c, fine_swaps[0], fine_nbr, fine_u, fine_swaps[1]
    )
    spreads[0].arrived()
    mate_places = copies.start(places.at[core], places.at[core], here.mate())
    fold_yz = one_hot_of(
        (1024, 256), lambda r, l: (r >> 6 == l >> 4) & ((r & 31) >> 1 == (l & 15))
    )
    fold_x = one_hot_of((16 * boxes, 32 * boxes), lambda r, l: l >> 1 == r)
    fine_swaps[1].arrived()
    live = count_ref[0, 0]
    residual_boxes(
        boxes,
        fine_u,
        fine_b,
        fine_d,
        fine_swaps[1],
        fine_nbr,
        rest_ref,
        lambda box: jnp.where(box < live, 1.0, 0.0).astype(F32),
    )
    cubes = pick_left(fold_x, pick_right(rest_ref[...], fold_yz)) * 0.5
    for box in range(boxes):
        octants[box] = cubes[16 * box : 16 * (box + 1)]

    def place_one(target, carry):
        slot = found_at[target]
        kept = jnp.where(slot >= 0, 1.0, 0.0).astype(F32)
        placed[target] = octants[jnp.maximum(slot, 0)] * kept
        return carry

    lax.fori_loop(0, 8 * n_node, place_one, 0)
    given = []
    for step, (other, device) in enumerate(here.peers_node()):
        given.append(
            copies.start(
                placed.at[pl.ds(pl.multiple_of(other * 8, 8), 8)], lifted.at[step], device
            )
        )
    spread = one_hot_of(
        (512, 512),
        lambda r, l: (r >> 8 == (l >> 4 & 1)) & ((r >> 4 & 15) == l >> 5) & ((r & 15) == (l & 15)),
    )
    inputs[1].wait()
    inputs[2].wait()
    arrived(given)
    total = placed[pl.ds(pl.multiple_of(here.node * 8, 8), 8)]
    for step in range(n_node - 1):
        total = total + lifted[step]
    pairs = jnp.concatenate(
        [jnp.concatenate([total[2 * k], total[2 * k + 1]], axis=1) for k in range(4)], axis=0
    )
    grown = pick_right(pairs, spread)
    for k in range(4):
        at_x, at_y = 16 * (k // 2), 512 * (k % 2)
        coarse_b[0, at_x : at_x + 16, at_y : at_y + 512] = (
            source_ref[0, at_x : at_x + 16, at_y : at_y + 512] + grown[16 * k : 16 * (k + 1)]
        )

    first_sweep(1, cu_first, coarse_b, coarse_d, coarse_c, coarse_swaps[0])
    coarse_swaps[0].arrived()
    sweep_boxes(
        1, cu_first, coarse_b, coarse_c, coarse_swaps[0], coarse_nbr, coarse_u, coarse_swaps[1]
    )
    fold_quarter = one_hot_of(
        (1024, 128), lambda r, l: (r >> 7 == (l >> 3 & 7)) & ((r >> 2 & 7) == ((l & 3) << 1) + (l >> 2 & 1))
    )
    coarse_swaps[1].arrived()
    residual_boxes(1, coarse_u, coarse_b, coarse_d, coarse_swaps[1], coarse_nbr, rest_ref)
    folded = pick_right(rest_ref[0:32], fold_quarter)
    early = pick_left(one_hot_of((8, 32), lambda r, l: l >> 2 == r), folded)
    late = pick_left(one_hot_of((8, 32), lambda r, l: l >> 2 == r + 4), folded)
    block = jnp.where(lanes_of((8, 128)) < 64, early, late) * 0.25
    blocks[core, 0] = block[0:4]

    spreads[1].start()
    arrived([mate_places])
    row = jnp.zeros((1, 128), I32)
    lane = lanes_of((1, 128))
    for number in range(n_box * n_node):
        row = jnp.where(lane == number, places[number // here.chips, number % here.chips], row)
    places_out[...] = row
    spreads[1].arrived()
    arrived([copies.start(blocks.at[core], blocks.at[core], here.mate())])
    blocks_out[...] = blocks[...]

    arrived(halo_x)
    copies.finish()
    for sent in fine_swaps + coarse_swaps + spreads:
        sent.finish()


def bottom_kernel(
    n_box, n_node, rows_x, rows_y, places, reach, blocks, out, scale, source, first, second, hits, sems
):
    deep, wide, long = reach.shape
    count = n_box * n_node
    per_side = long // 8
    side_bits = per_side.bit_length() - 1
    box, node = lax.axis_index("box"), lax.axis_index("node")
    at_x, at_y = box * rows_x - HALO, node * rows_y - Y_HALO
    fills = [
        pltpu.make_async_copy(
            reach.at[:, :, 128 * half : 128 * (half + 1)],
            scale.at[half, pl.ds(8, deep)],
            sems.at[half],
        )
        for half in range(2)
    ]
    for copy in fills:
        copy.start()
    zeros = jnp.zeros((wide, 128), F32)

    def clear(x, carry):
        for half in range(2):
            source[half, x] = zeros
            first[half, x] = zeros
        return carry

    lax.fori_loop(8, 8 + deep, clear, 0, unroll=2)
    out[...] = jnp.zeros(out.shape, F32)

    def where_is(number):
        place = places[0, number]
        return (
            (place >> 2 * side_bits << 3) - at_x,
            ((place >> side_bits & per_side - 1) << 3) - at_y,
            place & per_side - 1,
        )

    def look(number, found):
        x, y, _ = where_is(number)
        hits[found] = number
        hit = (x > -8) & (x < deep) & (y >= 0) & (y < wide)
        return found + hit.astype(I32)

    found = lax.fori_loop(0, count, look, jnp.int32(0), unroll=8)

    for copy in fills:
        copy.wait()

    def empty(x, carry):
        for half in range(2):
            scale[half, x] = zeros
        return carry

    lax.fori_loop(8, 8 + jnp.maximum(-at_x, 0), empty, 0)
    lax.fori_loop(8 + jnp.minimum(rows_x * n_box - at_x, deep), 8 + deep, empty, 0)

    def empty_rows(start):
        def one(x, carry):
            for half in range(2):
                scale[half, x, start : start + Y_HALO] = jnp.zeros((Y_HALO, 128), F32)
            return carry

        lax.fori_loop(8, 8 + deep, one, 0)

    pl.when(node == 0)(lambda: empty_rows(0))
    pl.when(node == n_node - 1)(lambda: empty_rows(Y_HALO + rows_y))

    lane, row = lanes_of((8, 128)), rows_of((8, 128))

    def fan_out(value, step):
        for bit in (1, 2, 4):
            value = jnp.where((row & bit) != 0, roll_lanes(value, step * bit), value)
        return value

    def put(at, carry):
        number = hits[at]
        x, y, z = where_is(number)
        block = blocks[number]
        kept = (lane >> 2) == z
        rows = pl.ds(pl.multiple_of(y, 8), 8)
        spots = [(half, x + ix + 8, rows) for half in range(2) for ix in range(8)]
        before = [source[spot] for spot in spots]
        first_before = [first[spot] for spot in spots]
        scales = [scale[spot] for spot in spots]
        fanned = [
            fan_out(jnp.broadcast_to(block[ix % 4 : ix % 4 + 1], (8, 128)), -8) for ix in range(8)
        ]
        fresh = []
        for half in range(2):
            for ix in range(8):
                shift = (z << 2) + 128 - 4 * half + 64 * (ix // 4) & 127
                fresh.append(jnp.where(kept, pltpu.roll(fanned[ix], shift, 1), 0.0))
        for number, spot in enumerate(spots):
            source[spot] = before[number] + fresh[number]
            first[spot] = first_before[number] + fresh[number] * scales[number]
        return carry

    lax.fori_loop(0, found, put, 0)

    refs = (first, second)
    eight = (8, 128)
    lane = lanes_of(eight)
    for sweep_no in range(HALO):
        left = HALO - 1 - sweep_no
        margin = (left + 3) // 4 * 4
        low = Y_HALO - margin
        here, there = refs[sweep_no % 2], refs[(sweep_no + 1) % 2]

        def plane(x, carry):
            fresh = []
            for at in range(low, low + rows_y + 2 * margin, 8):
                cut = slice(at, at + 8)
                mids = [here[half, x, cut, :] for half in range(2)]
                turned = (
                    jnp.where(lane == 0, 0.0, pltpu.roll(mids[1], 1, 1)),
                    jnp.where(lane == 127, 0.0, pltpu.roll(mids[0], 127, 1)),
                )
                for half in range(2):
                    around = here[half, x - 1, cut, :] + here[half, x + 1, cut, :]
                    around += here[half, x, at - 1 : at + 7, :] + here[half, x, at + 1 : at + 9, :]
                    around += mids[1 - half] + turned[half]
                    value = 0.2 * mids[half] + scale[half, x, cut, :] * (
                        source[half, x, cut, :] + around
                    )
                    fresh.append((half, cut, value))
            for half, cut, value in fresh:
                there[half, x, cut, :] = value
            return carry

        lax.fori_loop(8 + HALO - left, 8 + HALO + rows_x + left, plane, 0)
    solved = refs[HALO % 2]

    def take(at, carry):
        number = hits[at]
        x, y, z = where_is(number)

        @pl.when((x == HALO) & (y >= Y_HALO) & (y < Y_HALO + rows_y))
        def _():
            rows = pl.ds(pl.multiple_of(y, 8), 8)
            back = 128 - (z << 2)
            lines = []
            for ix in range(8):
                even, odd = [
                    pltpu.roll(
                        solved[half, 8 + HALO + ix, rows, :],
                        back + 4 * half + 64 * (ix // 4) & 127,
                        1,
                    )
                    for half in range(2)
                ]
                turned = fan_out(jnp.where((lane & 4) == 0, even, odd), 8)
                mine = jnp.where((lane >> 3) == row + 8 * (ix // 4), turned, 0.0)
                lines.append(jnp.sum(mine, axis=0, keepdims=True))
            for ix in range(4):
                out[number, ix : ix + 1] = lines[ix] + lines[ix + 4]

        return carry

    lax.fori_loop(0, found, take, 0)


def up_kernel(
    n_box,
    n_node,
    parts,
    fine_u,
    fine_c,
    fine_b,
    count_ref,
    fine_nbr,
    cover_ref,
    coarse_u,
    coarse_b,
    coarse_c,
    coarse_nbr,
    fine_out,
    coarse_out,
    from_core,
    sum_core,
    from_chips,
    own_block,
    cu_first,
    cu_second,
    yz_coarse_0,
    x_coarse_0,
    yz_coarse_1,
    x_coarse_1,
    octants,
    picked,
    u_first,
    u_second,
    yz_fine_0,
    x_fine_0,
    yz_fine_1,
    x_fine_1,
    send_sems,
    recv_sems,
    fine_sent,
    fine_came,
    coarse_sent,
    coarse_came,
    spread_sent,
    spread_came,
):
    here = Place(n_box, n_node)
    copies = Copies(send_sems, recv_sems)
    boxes = fine_u.shape[0]
    core = here.core
    fine_swaps = [
        Swap(here, yz, x, boxes, 2, fine_sent.at[number], fine_came.at[number])
        for number, (yz, x) in enumerate(((yz_fine_0, x_fine_0), (yz_fine_1, x_fine_1)))
    ]
    coarse_swaps = [
        Swap(here, yz, x, 1, 1, coarse_sent.at[number], coarse_came.at[number])
        for number, (yz, x) in enumerate(((yz_coarse_0, x_coarse_0), (yz_coarse_1, x_coarse_1)))
    ]
    here.greet([])
    here.greeted()

    arrived([copies.start(parts.at[1 - core], from_core, here.mate())])
    sum_core[...] = parts[core] + from_core[...]
    spread = Spread(
        here,
        lambda step: sum_core.at[step],
        lambda step: from_chips.at[step],
        here.before_chip,
        spread_sent,
        spread_came,
    )
    from_chips[0] = sum_core[0]
    spread.start()
    grow_quarter = one_hot_of(
        (128, 1024), lambda r, l: r == (l >> 7 << 3) + (l >> 3 & 3) + (l >> 2 & 1) * 4
    )
    spread.arrived()
    block = jnp.sum(from_chips[...], axis=0)
    own_block[0:4] = block
    own_block[4:8] = pltpu.roll(block, 64, 1)
    grown = pick_right(own_block[...], grow_quarter)
    grown = pick_left(one_hot_of((32, 8), lambda r, l: r >> 2 == l), grown)
    cu_first[0] = coarse_u[0] + grown
    put_faces(tiles_of(cu_first, 0), yz_coarse_0, x_coarse_0, 1)
    coarse_swaps[0].start(0)
    coarse_swaps[0].arrived()
    sweep_boxes(
        1, cu_first, coarse_b, coarse_c, coarse_swaps[0], coarse_nbr, cu_second, coarse_swaps[1]
    )
    split = one_hot_of(
        (512, 512),
        lambda r, l: (l >> 8 == (r >> 4 & 1)) & ((l >> 4 & 15) == r >> 5) & ((l & 15) == (r & 15)),
    )
    coarse_swaps[1].arrived()
    sweep_boxes(
        1, cu_second, coarse_b, coarse_c, coarse_swaps[1], coarse_nbr, coarse_out, None
    )

    quarters = jnp.concatenate(
        [
            coarse_out[0, 16 * (k // 2) : 16 * (k // 2) + 16, 512 * (k % 2) : 512 * (k % 2) + 512]
            for k in range(4)
        ],
        axis=0,
    )
    cubes = pick_right(quarters, split)
    base = pl.multiple_of(here.node * 8, 8)
    for k in range(8):
        octants[base + k] = cubes[16 * (k // 2) : 16 * (k // 2) + 16, 256 * (k % 2) : 256 * (k % 2) + 256]
    own = octants.at[pl.ds(base, 8)]
    waits = [copies.start(own, own, device) for _, device in here.peers_node()]
    grow_yz = one_hot_of(
        (256, 1024), lambda r, l: (l >> 6 == r >> 4) & ((l >> 1 & 15) == (r & 15))
    )
    grow_x = one_hot_of((32 * boxes, 16 * boxes), lambda r, l: r >> 1 == l)
    arrived(waits)
    for box in range(boxes):
        picked[16 * box : 16 * (box + 1)] = octants[cover_ref[0, box]]
    tall = pick_right(pick_left(grow_x, picked[...]), grow_yz)
    for box in range(boxes):
        u_first[box] = fine_u[box] + tall[32 * box : 32 * (box + 1)]

    def faces_of(box, carry):
        put_faces(tiles_of(u_first, box), yz_fine_0, x_fine_0, boxes + box)

    by_chunks(boxes, fine_swaps[0], faces_of)
    fine_swaps[0].arrived()
    sweep_boxes(
        boxes, u_first, fine_b, fine_c, fine_swaps[0], fine_nbr, u_second, fine_swaps[1]
    )
    fine_swaps[1].arrived()
    live = count_ref[0, 0]
    sweep_boxes(
        boxes,
        u_second,
        fine_b,
        fine_c,
        fine_swaps[1],
        fine_nbr,
        fine_out,
        None,
        lambda box: jnp.where(box < live, 1.0, 0.0).astype(F32),
    )
    copies.finish()
    for sent in fine_swaps + coarse_swaps + [spread]:
        sent.finish()


VMEM, SMEM, ANY = (
    pl.BlockSpec(memory_space=pltpu.VMEM),
    pl.BlockSpec(memory_space=pltpu.SMEM),
    pl.BlockSpec(memory_space=pl.ANY),
)


def shards(
    n_box,
    n_node,
    fine_rhs,
    fine_diag,
    fine_count,
    fine_nbr,
    fine_cover,
    coarse_source,
    coarse_diag,
    coarse_nbr,
    coarse_place,
    bottom_diag,
):
    boxes = fine_rhs.shape[0]
    ny, nz, nc = grid_of(n_box)
    rows_x, rows_y, long = bottom_diag.shape
    deep, wide = rows_x + 2 * HALO, rows_y + 2 * Y_HALO
    count = n_box * n_node

    def like(shape, kind=F32):
        return jax.ShapeDtypeStruct(shape, kind)

    fine, coarse = (boxes, 32, 1024), (1, 32, 1024)
    chips = ny * nz * n_node
    grid = (nc, chips)
    limit = 48 * 1024 * 1024
    fine_u, fine_c, coarse_u, coarse_b, coarse_c, reach, blocks, places = pl.pallas_call(
        functools.partial(down_kernel, n_box, n_node),
        out_shape=(
            like(fine),
            like(fine),
            like(coarse),
            like(coarse),
            like(coarse),
            like((deep, wide, long)),
            like(grid + (4, 128)),
            like((1, 128), I32),
        ),
        in_specs=[ANY, ANY, SMEM, SMEM, SMEM, ANY, ANY, SMEM, SMEM, ANY],
        out_specs=(VMEM, VMEM, VMEM, VMEM, VMEM, ANY, VMEM, VMEM),
        scratch_shapes=[
            pltpu.VMEM(fine, F32),
            pltpu.VMEM(fine, F32),
            pltpu.VMEM(coarse, F32),
            pltpu.VMEM(coarse, F32),
            pltpu.VMEM((rows_x, rows_y, long), F32),
            pltpu.VMEM(fine, F32),
            pltpu.VMEM((3 * boxes, 32, 128), F32),
            pltpu.VMEM((3 * boxes, 2, 1024), F32),
            pltpu.VMEM((3 * boxes, 32, 128), F32),
            pltpu.VMEM((3 * boxes, 2, 1024), F32),
            pltpu.VMEM((rows_x, rows_y, long), F32),
            pltpu.VMEM((32 * boxes, 1024), F32),
            pltpu.VMEM((boxes, 16, 256), F32),
            pltpu.VMEM((8 * n_node, 16, 256), F32),
            pltpu.VMEM((n_node - 1, 8, 16, 256), F32),
            pltpu.SMEM((8 * n_node,), I32),
            pltpu.VMEM(coarse, F32),
            pltpu.VMEM((3, 32, 128), F32),
            pltpu.VMEM((3, 2, 1024), F32),
            pltpu.VMEM((3, 32, 128), F32),
            pltpu.VMEM((3, 2, 1024), F32),
            pltpu.VMEM(grid + (4, 128), F32),
            pltpu.VMEM(grid + (1, 128), I32),
            pltpu.SemaphoreType.DMA((64,)),
            pltpu.SemaphoreType.DMA((64,)),
            pltpu.SemaphoreType.DMA,
            pltpu.SemaphoreType.DMA((2, boxes)),
            pltpu.SemaphoreType.DMA((3,)),
            pltpu.SemaphoreType.DMA((2, boxes // 2, 4)),
            pltpu.SemaphoreType.DMA((2, boxes // 2, 4)),
            pltpu.SemaphoreType.DMA((2, 1, 4)),
            pltpu.SemaphoreType.DMA((2, 1, 4)),
            pltpu.SemaphoreType.DMA((2, chips)),
            pltpu.SemaphoreType.DMA((2, chips)),
        ],
        compiler_params=pltpu.CompilerParams(
            collective_id=0, has_side_effects=True, vmem_limit_bytes=limit
        ),
        name="down",
    )(
        fine_rhs,
        fine_diag,
        fine_count,
        fine_nbr,
        fine_cover,
        coarse_source,
        coarse_diag,
        coarse_nbr,
        coarse_place,
        bottom_diag,
    )
    parts = pl.pallas_call(
        functools.partial(bottom_kernel, n_box, n_node, rows_x, rows_y),
        out_shape=like((count, 4, 128)),
        in_specs=[SMEM, ANY, VMEM],
        out_specs=VMEM,
        scratch_shapes=[
            pltpu.VMEM((2, deep + 16, wide, 128), F32),
            pltpu.VMEM((2, deep + 16, wide, 128), F32),
            pltpu.VMEM((2, deep + 16, wide, 128), F32),
            pltpu.VMEM((2, deep + 16, wide, 128), F32),
            pltpu.SMEM((count + 1,), I32),
            pltpu.SemaphoreType.DMA((2,)),
        ],
        compiler_params=pltpu.CompilerParams(vmem_limit_bytes=limit),
        name="bottom",
    )(places, reach, blocks.reshape(count, 4, 128))
    fine_out, coarse_out = pl.pallas_call(
        functools.partial(up_kernel, n_box, n_node),
        out_shape=(like(fine), like(coarse)),
        in_specs=[VMEM, VMEM, VMEM, VMEM, SMEM, SMEM, SMEM, VMEM, VMEM, VMEM, SMEM],
        out_specs=(VMEM, VMEM),
        scratch_shapes=[
            pltpu.VMEM((chips, 4, 128), F32),
            pltpu.VMEM((chips, 4, 128), F32),
            pltpu.VMEM((chips, 4, 128), F32),
            pltpu.VMEM((8, 128), F32),
            pltpu.VMEM(coarse, F32),
            pltpu.VMEM(coarse, F32),
            pltpu.VMEM((3, 32, 128), F32),
            pltpu.VMEM((3, 2, 1024), F32),
            pltpu.VMEM((3, 32, 128), F32),
            pltpu.VMEM((3, 2, 1024), F32),
            pltpu.VMEM((8 * n_node, 16, 256), F32),
            pltpu.VMEM((16 * boxes, 256), F32),
            pltpu.VMEM(fine, F32),
            pltpu.VMEM(fine, F32),
            pltpu.VMEM((3 * boxes, 32, 128), F32),
            pltpu.VMEM((3 * boxes, 2, 1024), F32),
            pltpu.VMEM((3 * boxes, 32, 128), F32),
            pltpu.VMEM((3 * boxes, 2, 1024), F32),
            pltpu.SemaphoreType.DMA((8,)),
            pltpu.SemaphoreType.DMA((8,)),
            pltpu.SemaphoreType.DMA((2, boxes // 2, 4)),
            pltpu.SemaphoreType.DMA((2, boxes // 2, 4)),
            pltpu.SemaphoreType.DMA((2, 1, 4)),
            pltpu.SemaphoreType.DMA((2, 1, 4)),
            pltpu.SemaphoreType.DMA((chips,)),
            pltpu.SemaphoreType.DMA((chips,)),
        ],
        compiler_params=pltpu.CompilerParams(
            collective_id=1, has_side_effects=True, vmem_limit_bytes=limit
        ),
        name="up",
    )(
        parts.reshape(grid + (4, 128)),
        fine_u,
        fine_c,
        fine_rhs,
        fine_count,
        fine_nbr,
        fine_cover,
        coarse_u,
        coarse_b,
        coarse_c,
        coarse_nbr,
    )
    return fine_out, coarse_out


def solution(mesh):
    n_box, n_node = mesh.shape["box"], mesh.shape["node"]
    return jax.shard_map(
        functools.partial(shards, n_box, n_node),
        mesh=mesh,
        in_specs=(
            P(("box", "node"), None, None),
            P(("box", "node"), None, None),
            P("box", "node"),
            P(("box", "node"), None),
            P("box", "node"),
            P(("box", "node"), None, None),
            P(("box", "node"), None, None),
            P(("box", "node"), None),
            P(("box", "node")),
            P("box", "node", None),
        ),
        out_specs=(P(("box", "node"), None, None), P(("box", "node"), None, None)),
        check_vma=False,
    )
```

time: 168 us -> 158 us (0.940)
  Pallas kernels: 155 us -> 145 us
    pallas_call x1, Pallas kernels: 34.3 us -> 21.7 us  [shards(): pl.pallas_call(functools.partial(bottom_kernel, n_box, n_node, rows_x, ro...]
    pallas_call x1, Pallas kernels: 60.4 us -> 65.6 us  [shards(): pl.pallas_call(functools.partial(down_kernel, n_box, n_node), out_shape=(...]
    pallas_call x1, Pallas kernels: 60 us -> 57.9 us  [shards(): pl.pallas_call(functools.partial(up_kernel, n_box, n_node), out_shape=(li...]
where the time goes in v2:
time: 158 us
  Pallas kernels  145 us (92%)
  local copies, waits for them, and re-layouts  10.8 us (7%)
  between operations  2.01 us (1%)
    pallas_call x1, Pallas kernels, shards(): pl.pallas_call(functools.partial(down_kernel, n_box, n_node), out_shape=(...  65.6 us
    pallas_call x1, Pallas kernels, shards(): pl.pallas_call(functools.partial(up_kernel, n_box, n_node), out_shape=(li...  57.9 us
    pallas_call x1, Pallas kernels, shards(): pl.pallas_call(functools.partial(bottom_kernel, n_box, n_node, rows_x, ro...  21.7 us
    unnamed x28, local copies, waits for them, and re-layouts  10.8 us

profile of v2, /device:TPU:0, one launch (start us, length us, event | category | flops | bytes accessed | tf_op | source)
XLA Modules:
  0.0 157.9 jit_solution(745732667066153738)
XLA Ops:
  1.9 0.0 copy-start
  1.9 1.2 copy-done
  3.2 0.0 copy-start.3
  3.2 1.2 copy-done.3
  4.4 0.0 copy-start.4
  4.4 1.0 copy-done.4
  5.4 0.0 copy-start.5
  5.4 0.9 copy-done.5
  6.3 0.0 copy-start.6
  6.3 0.9 copy-done.6
  7.2 0.0 copy-start.7
  7.2 0.7 copy-done.7
  7.9 0.0 copy-start.9
  7.9 0.7 copy-done.9
  8.6 0.0 copy-start.11
  8.6 0.7 copy-done.11
  9.2 0.0 copy-start.1
  9.2 0.0 copy-start.8
  9.2 0.0 copy-start.10
  9.2 0.0 copy-start.12
  9.2 65.6 %down.1 = (f32[8,32,1024]{2,1,0:T(8,128)S(1)}, f32[8,32,1024]{2,1,0:T(8,128)S(1)}, f32[1,32,1024]{2,1,0:T(8,128)S(1)}, f32[1,32,1024]{2,1,0:T(8,128)S(1)}, f32[1...) custom-call(f32[8,32,1024]{2,1,0:T(8,128)S(1)} %copy-done, ...), custom_call_target="tpu_custom_call" | custom-call | tf_op jit(solution)/shard_map/down/pallas_call | solution.py:984
  74.8 0.0 copy-start.2
  74.8 1.8 %copy-done.2 = f32[30,96,256]{2,1,0:T(8,128)S(1)} copy-done((f32[30,96,256]{2,1,0:T(8,128)S(1)}, f32[30,96,256]{2,1,0:T(8,128)}, u32[]{:S(2)}) %copy-start.2) | copy-done | bytes 2949144
  76.7 21.7 %bottom.1 = f32[128,4,128]{2,1,0:T(4,128)S(1)} custom-call(s32[1,128]{1,0:T(1,128)S(1)} %get-tuple-element.10.places, f32[30,96,256]{2,1,0:T(8,128)S(1)} %copy-done.2, f32[128,4,128]{2,1,0:T(4,128)S(1)} %bitcast.3), custom_call_target="tpu_custom_call" | custom-call | tf_op jit(solution)/shard_map/bottom/pallas_call | solution.py:1050
  98.4 0.0 copy-done.1
  98.4 0.0 copy-done.8
  98.4 0.0 copy-done.10
  98.4 0.0 copy-done.12
  98.4 57.9 %up.1 = (f32[8,32,1024]{2,1,0:T(8,128)S(1)}, f32[1,32,1024]{2,1,0:T(8,128)S(1)}) custom-call(f32[2,64,4,128]{3,2,1,0:T(4,128)S(1)} %bitcast.2, f32[8,32,1024]{2,1,0:T(8,128)S(1)} %get-tuple-element.13.fine_u, f32[8,32,1024]{2,1,0:T(8,128)S(1)} %get-tuple-element.14.fine_c, f32[8,32,1024]{2,1,0:T(8,128)S(1)} %copy-done.1, s32[1,1]{1,0:T(1,128)S(6)} %copy.14.count_ref, ...), custom_call_target="tpu_custom_call" | custom-call | tf_op jit(solution)/shard_map/up/pallas_call | solution.py:1066
  156.3 1.0 copy.16
  157.3 0.7 copy.17
Async XLA Ops:
  1.9 1.2 copy-start
  3.2 1.2 copy-start.3
  4.4 1.0 copy-start.4
  5.4 0.9 copy-start.5
  6.3 0.9 copy-start.6
  7.2 0.7 copy-start.7
  7.9 0.7 copy-start.9
  8.6 0.7 copy-start.11
  9.2 89.1 %copy-start.1 = (f32[8,32,1024]{2,1,0:T(8,128)S(1)}, f32[8,32,1024]{2,1,0:T(8,128)}, u32[]{:S(2)}) copy-start(f32[8,32,1024]{2,1,0:T(8,128)} %fine_b.1) | copy-start | bytes 3145732
  9.2 89.2 %copy-start.8 = (s32[8,6]{1,0:T(8,128)S(1)}, s32[8,6]{1,0:T(8,128)}, u32[]{:S(2)}) copy-start(s32[8,6]{1,0:T(8,128)} %fine_nbr.3) | copy-start | bytes 580
  9.2 89.2 %copy-start.10 = (s32[1,8]{1,0:T(1,128)S(1)}, s32[1,8]{1,0:T(1,128)}, u32[]{:S(2)}) copy-start(s32[1,8]{1,0:T(1,128)} %cover_ref.3) | copy-start | bytes 100
  9.2 89.2 %copy-start.12 = (s32[1,6]{1,0:T(1,128)S(1)}, s32[1,6]{1,0:T(1,128)}, u32[]{:S(2)}) copy-start(s32[1,6]{1,0:T(1,128)} %coarse_nbr.3) | copy-start | bytes 76
  74.8 1.8 %copy-start.2 = (f32[30,96,256]{2,1,0:T(8,128)S(1)}, f32[30,96,256]{2,1,0:T(8,128)}, u32[]{:S(2)}) copy-start(f32[30,96,256]{2,1,0:T(8,128)} %get-tuple-element.11.reach) | copy-start | bytes 8847364

commit v3 on v2

--- a/solution.py
+++ b/solution.py
@@ -12,6 +12,7 @@
 BOT_ITERS = 12
 HALO = BOT_ITERS - 1
 Y_HALO = 16
+AT_ONCE = 4
 TILES = 8
 
 
@@ -142,6 +143,22 @@
     return sums
 
 
+def fan_out(value, step):
+    row = rows_of((8, 128))
+    for bit in (1, 2, 4):
+        value = jnp.where((row & bit) != 0, roll_lanes(value, step * bit), value)
+    return value
+
+
+def swap_eights(value):
+    lane = lanes_of((8, 128))
+    result = jnp.zeros((8, 128), F32)
+    for b in range(8):
+        spread = fan_out(jnp.broadcast_to(value[b : b + 1], (8, 128)), -8)
+        result = jnp.where((lane >> 3) == b, roll_lanes(spread, 8 * b), result)
+    return result
+
+
 class Copies:
     def __init__(self, send_sems, recv_sems):
         self.send_sems, self.recv_sems, self.made = send_sems, recv_sems, []
@@ -281,7 +298,7 @@
     def some(chunk, carry):
         for number in range(step):
             one(chunk * step + number, 0)
-        if swap is not None:
+        if swap is not None and swap.step == step:
             swap.start(chunk)
         return carry
 
@@ -386,21 +403,29 @@
     fine_b_in,
     fine_d_in,
     count_ref,
-    fine_nbr,
-    cover_ref,
+    nbr_in,
+    cover_in,
     source_in,
     coarse_d_in,
-    coarse_nbr,
+    coarse_nbr_in,
     place_ref,
     bottom_d_in,
+    fine_u_out,
+    fine_c_out,
+    coarse_u_out,
+    coarse_b_out,
+    coarse_c_out,
+    reach,
+    blocks_out,
+    places_out,
     fine_u,
     fine_c,
     coarse_u,
     coarse_b,
     coarse_c,
-    reach,
-    blocks_out,
-    places_out,
+    fine_nbr,
+    cover_ref,
+    coarse_nbr,
     fine_b,
     fine_d,
     source_ref,
@@ -429,6 +454,7 @@
     local_sem,
     fine_sems,
     input_sems,
+    output_sems,
     fine_sent,
     fine_came,
     coarse_sent,
@@ -450,13 +476,25 @@
     inputs = [
         pltpu.make_async_copy(source, target, input_sems.at[number])
         for number, (source, target) in enumerate(
-            ((bottom_d_in, bottom_d), (source_in, source_ref), (coarse_d_in, coarse_d))
+            (
+                (bottom_d_in, bottom_d),
+                (source_in, source_ref),
+                (coarse_d_in, coarse_d),
+                (nbr_in, fine_nbr),
+                (cover_in, cover_ref),
+                (coarse_nbr_in, coarse_nbr),
+            )
         )
     ]
     for copy in inputs:
         copy.start()
     here.greet([here.at_box(1), here.at_box(-1), here.at_box(2), here.at_box(-2)])
 
+    def keep(source, target, number):
+        copy = pltpu.make_async_copy(source, target, output_sems.at[number])
+        copy.start()
+        return copy
+
     def ready(box):
         fine_input(box, 0).wait()
         fine_input(box, 1).wait()
@@ -464,8 +502,10 @@
     core = here.core
     places[core, 0] = jnp.full((1, 128), place_ref[0], I32)
     fine_swaps = [
-        Swap(here, yz, x, boxes, 2, fine_sent.at[number], fine_came.at[number])
-        for number, (yz, x) in enumerate(((yz_fine_0, x_fine_0), (yz_fine_1, x_fine_1)))
+        Swap(here, yz, x, boxes, step, fine_sent.at[number], fine_came.at[number])
+        for number, (yz, x, step) in enumerate(
+            ((yz_fine_0, x_fine_0, boxes), (yz_fine_1, x_fine_1, 2))
+        )
     ]
     coarse_swaps = [
         Swap(here, yz, x, 1, 1, coarse_sent.at[number], coarse_came.at[number])
@@ -483,12 +523,10 @@
         for number, ref in enumerate((places, blocks))
     ]
 
-    here.greeted()
     first_sweep(boxes, u_first, fine_b, fine_d, fine_c, fine_swaps[0], ready)
-
+    kept = [keep(fine_c, fine_c_out, 0)]
     rows_x, rows_y = bottom_d.shape[0], bottom_d.shape[1]
     inputs[0].wait()
-
     part_z = one_hot_of((256, 256), lambda r, l: r == ((l & 127) << 1) + (l >> 7))
 
     def scale_plane(x, carry):
@@ -496,6 +534,8 @@
         return carry
 
     lax.fori_loop(0, rows_x, scale_plane, 0)
+    here.greeted()
+    fine_swaps[0].start(0)
     own_x, own_y = pl.ds(HALO, rows_x), pl.ds(Y_HALO, rows_y)
     own_copy = pltpu.make_async_copy(slab_c, reach.at[own_x, own_y], local_sem)
     own_copy.start()
@@ -529,6 +569,8 @@
     ]
     spreads[0].start()
 
+    for copy in inputs[1:]:
+        copy.wait()
     for target in range(8 * n_node):
         slot = jnp.int32(-1)
         for box in range(boxes):
@@ -551,6 +593,7 @@
     sweep_boxes(
         boxes, u_first, fine_b, fine_c, fine_swaps[0], fine_nbr, fine_u, fine_swaps[1]
     )
+    kept.append(keep(fine_u, fine_u_out, 1))
     spreads[0].arrived()
     mate_places = copies.start(places.at[core], places.at[core], here.mate())
     fold_yz = one_hot_of(
@@ -591,8 +634,6 @@
         (512, 512),
         lambda r, l: (r >> 8 == (l >> 4 & 1)) & ((r >> 4 & 15) == l >> 5) & ((r & 15) == (l & 15)),
     )
-    inputs[1].wait()
-    inputs[2].wait()
     arrived(given)
     total = placed[pl.ds(pl.multiple_of(here.node * 8, 8), 8)]
     for step in range(n_node - 1):
@@ -608,20 +649,22 @@
         )
 
     first_sweep(1, cu_first, coarse_b, coarse_d, coarse_c, coarse_swaps[0])
+    kept += [keep(coarse_b, coarse_b_out, 2), keep(coarse_c, coarse_c_out, 3)]
     coarse_swaps[0].arrived()
     sweep_boxes(
         1, cu_first, coarse_b, coarse_c, coarse_swaps[0], coarse_nbr, coarse_u, coarse_swaps[1]
     )
+    kept.append(keep(coarse_u, coarse_u_out, 4))
     fold_quarter = one_hot_of(
         (1024, 128), lambda r, l: (r >> 7 == (l >> 3 & 7)) & ((r >> 2 & 7) == ((l & 3) << 1) + (l >> 2 & 1))
     )
     coarse_swaps[1].arrived()
     residual_boxes(1, coarse_u, coarse_b, coarse_d, coarse_swaps[1], coarse_nbr, rest_ref)
     folded = pick_right(rest_ref[0:32], fold_quarter)
-    early = pick_left(one_hot_of((8, 32), lambda r, l: l >> 2 == r), folded)
-    late = pick_left(one_hot_of((8, 32), lambda r, l: l >> 2 == r + 4), folded)
-    block = jnp.where(lanes_of((8, 128)) < 64, early, late) * 0.25
-    blocks[core, 0] = block[0:4]
+    folded = pick_left(one_hot_of((8, 32), lambda r, l: l >> 2 == r), folded) * 0.25
+    block = swap_eights(folded)
+    late = pltpu.roll(block, 64, 1)
+    blocks[core, 0] = jnp.where(lanes_of((4, 128)) < 64, block[0:4], late[4:8])
 
     spreads[1].start()
     arrived([mate_places])
@@ -632,16 +675,17 @@
     places_out[...] = row
     spreads[1].arrived()
     arrived([copies.start(blocks.at[core], blocks.at[core], here.mate())])
-    blocks_out[...] = blocks[...]
-
+    kept.append(keep(blocks, blocks_out, 5))
     arrived(halo_x)
     copies.finish()
+    for copy in kept:
+        copy.wait()
     for sent in fine_swaps + coarse_swaps + spreads:
         sent.finish()
 
 
 def bottom_kernel(
-    n_box, n_node, rows_x, rows_y, places, reach, blocks, out, scale, source, first, second, hits, sems
+    n_box, n_node, rows_x, rows_y, places, reach, blocks_in, out, blocks, scale, source, first, second, hits, sems
 ):
     deep, wide, long = reach.shape
     count = n_box * n_node
@@ -657,6 +701,7 @@
         )
         for half in range(2)
     ]
+    fills.append(pltpu.make_async_copy(blocks_in, blocks, sems.at[2]))
     for copy in fills:
         copy.start()
     zeros = jnp.zeros((wide, 128), F32)
@@ -709,11 +754,6 @@
     pl.when(node == n_node - 1)(lambda: empty_rows(Y_HALO + rows_y))
 
     lane, row = lanes_of((8, 128)), rows_of((8, 128))
-
-    def fan_out(value, step):
-        for bit in (1, 2, 4):
-            value = jnp.where((row & bit) != 0, roll_lanes(value, step * bit), value)
-        return value
 
     def put(at, carry):
         number = hits[at]
@@ -725,14 +765,12 @@
         before = [source[spot] for spot in spots]
         first_before = [first[spot] for spot in spots]
         scales = [scale[spot] for spot in spots]
-        fanned = [
-            fan_out(jnp.broadcast_to(block[ix % 4 : ix % 4 + 1], (8, 128)), -8) for ix in range(8)
-        ]
+        whole = jnp.concatenate([block, pltpu.roll(block, 64, 1)], axis=0)
         fresh = []
         for half in range(2):
             for ix in range(8):
-                shift = (z << 2) + 128 - 4 * half + 64 * (ix // 4) & 127
-                fresh.append(jnp.where(kept, pltpu.roll(fanned[ix], shift, 1), 0.0))
+                shift = (z << 2) + 128 - 4 * half - 8 * ix & 127
+                fresh.append(jnp.where(kept, pltpu.roll(whole, shift, 1), 0.0))
         for number, spot in enumerate(spots):
             source[spot] = before[number] + fresh[number]
             first[spot] = first_before[number] + fresh[number] * scales[number]
@@ -749,28 +787,31 @@
         low = Y_HALO - margin
         here, there = refs[sweep_no % 2], refs[(sweep_no + 1) % 2]
 
-        def plane(x, carry):
+        def planes(group, carry):
             fresh = []
-            for at in range(low, low + rows_y + 2 * margin, 8):
-                cut = slice(at, at + 8)
-                mids = [here[half, x, cut, :] for half in range(2)]
-                turned = (
-                    jnp.where(lane == 0, 0.0, pltpu.roll(mids[1], 1, 1)),
-                    jnp.where(lane == 127, 0.0, pltpu.roll(mids[0], 127, 1)),
-                )
-                for half in range(2):
-                    around = here[half, x - 1, cut, :] + here[half, x + 1, cut, :]
-                    around += here[half, x, at - 1 : at + 7, :] + here[half, x, at + 1 : at + 9, :]
-                    around += mids[1 - half] + turned[half]
-                    value = 0.2 * mids[half] + scale[half, x, cut, :] * (
-                        source[half, x, cut, :] + around
+            for number in range(AT_ONCE):
+                x = 8 + HALO - left + AT_ONCE * group + number
+                for at in range(low, low + rows_y + 2 * margin, 8):
+                    cut = slice(at, at + 8)
+                    mids = [here[half, x, cut, :] for half in range(2)]
+                    turned = (
+                        jnp.where(lane == 0, 0.0, pltpu.roll(mids[1], 1, 1)),
+                        jnp.where(lane == 127, 0.0, pltpu.roll(mids[0], 127, 1)),
                     )
-                    fresh.append((half, cut, value))
-            for half, cut, value in fresh:
+                    for half in range(2):
+                        around = here[half, x - 1, cut, :] + here[half, x + 1, cut, :]
+                        around += here[half, x, at - 1 : at + 7, :]
+                        around += here[half, x, at + 1 : at + 9, :]
+                        around += mids[1 - half] + turned[half]
+                        value = 0.2 * mids[half] + scale[half, x, cut, :] * (
+                            source[half, x, cut, :] + around
+                        )
+                        fresh.append((half, x, cut, value))
+            for half, x, cut, value in fresh:
                 there[half, x, cut, :] = value
             return carry
 
-        lax.fori_loop(8 + HALO - left, 8 + HALO + rows_x + left, plane, 0)
+        lax.fori_loop(0, (rows_x + 2 * left + AT_ONCE - 1) // AT_ONCE, planes, 0)
     solved = refs[HALO % 2]
 
     def take(at, carry):
@@ -781,21 +822,15 @@
         def _():
             rows = pl.ds(pl.multiple_of(y, 8), 8)
             back = 128 - (z << 2)
-            lines = []
+            gathered = jnp.zeros(eight, F32)
             for ix in range(8):
-                even, odd = [
-                    pltpu.roll(
-                        solved[half, 8 + HALO + ix, rows, :],
-                        back + 4 * half + 64 * (ix // 4) & 127,
-                        1,
+                for half in range(2):
+                    turned = pltpu.roll(
+                        solved[half, 8 + HALO + ix, rows, :], back + 4 * half + 8 * ix & 127, 1
                     )
-                    for half in range(2)
-                ]
-                turned = fan_out(jnp.where((lane & 4) == 0, even, odd), 8)
-                mine = jnp.where((lane >> 3) == row + 8 * (ix // 4), turned, 0.0)
-                lines.append(jnp.sum(mine, axis=0, keepdims=True))
-            for ix in range(4):
-                out[number, ix : ix + 1] = lines[ix] + lines[ix + 4]
+                    gathered = jnp.where((lane >> 2) == 2 * ix + half, turned, gathered)
+            late = pltpu.roll(gathered, 64, 1)
+            out[number] = jnp.where(lanes_of((4, 128)) < 64, gathered[0:4], late[4:8])
 
         return carry
 
@@ -805,19 +840,30 @@
 def up_kernel(
     n_box,
     n_node,
-    parts,
+    parts_in,
+    fine_u_in,
+    fine_c_in,
+    fine_b_in,
+    count_ref,
+    nbr_in,
+    cover_in,
+    coarse_u_in,
+    coarse_b_in,
+    coarse_c_in,
+    coarse_nbr_in,
+    fine_out,
+    coarse_out,
     fine_u,
     fine_c,
     fine_b,
-    count_ref,
     fine_nbr,
     cover_ref,
     coarse_u,
     coarse_b,
     coarse_c,
     coarse_nbr,
-    fine_out,
-    coarse_out,
+    own_parts,
+    input_sems,
     from_core,
     sum_core,
     from_chips,
@@ -849,6 +895,25 @@
     copies = Copies(send_sems, recv_sems)
     boxes = fine_u.shape[0]
     core = here.core
+    inputs = [
+        pltpu.make_async_copy(source, target, input_sems.at[number])
+        for number, (source, target) in enumerate(
+            (
+                (parts_in.at[core], own_parts),
+                (coarse_u_in, coarse_u),
+                (coarse_b_in, coarse_b),
+                (coarse_c_in, coarse_c),
+                (coarse_nbr_in, coarse_nbr),
+                (nbr_in, fine_nbr),
+                (cover_in, cover_ref),
+                (fine_u_in, fine_u),
+                (fine_c_in, fine_c),
+                (fine_b_in, fine_b),
+            )
+        )
+    ]
+    for copy in inputs:
+        copy.start()
     fine_swaps = [
         Swap(here, yz, x, boxes, 2, fine_sent.at[number], fine_came.at[number])
         for number, (yz, x) in enumerate(((yz_fine_0, x_fine_0), (yz_fine_1, x_fine_1)))
@@ -860,8 +925,11 @@
     here.greet([])
     here.greeted()
 
-    arrived([copies.start(parts.at[1 - core], from_core, here.mate())])
-    sum_core[...] = parts[core] + from_core[...]
+    from_mate = copies.start(parts_in.at[1 - core], from_core, here.mate())
+    for copy in inputs:
+        copy.wait()
+    arrived([from_mate])
+    sum_core[...] = own_parts[...] + from_core[...]
     spread = Spread(
         here,
         lambda step: sum_core.at[step],
@@ -879,7 +947,7 @@
     block = jnp.sum(from_chips[...], axis=0)
     own_block[0:4] = block
     own_block[4:8] = pltpu.roll(block, 64, 1)
-    grown = pick_right(own_block[...], grow_quarter)
+    grown = pick_right(swap_eights(own_block[...]), grow_quarter)
     grown = pick_left(one_hot_of((32, 8), lambda r, l: r >> 2 == l), grown)
     cu_first[0] = coarse_u[0] + grown
     put_faces(tiles_of(cu_first, 0), yz_coarse_0, x_coarse_0, 1)
@@ -980,7 +1048,7 @@
     fine, coarse = (boxes, 32, 1024), (1, 32, 1024)
     chips = ny * nz * n_node
     grid = (nc, chips)
-    limit = 48 * 1024 * 1024
+    limit = 62 * 1024 * 1024
     fine_u, fine_c, coarse_u, coarse_b, coarse_c, reach, blocks, places = pl.pallas_call(
         functools.partial(down_kernel, n_box, n_node),
         out_shape=(
@@ -993,9 +1061,17 @@
             like(grid + (4, 128)),
             like((1, 128), I32),
         ),
-        in_specs=[ANY, ANY, SMEM, SMEM, SMEM, ANY, ANY, SMEM, SMEM, ANY],
-        out_specs=(VMEM, VMEM, VMEM, VMEM, VMEM, ANY, VMEM, VMEM),
+        in_specs=[ANY, ANY, SMEM, ANY, ANY, ANY, ANY, ANY, SMEM, ANY],
+        out_specs=(ANY, ANY, ANY, ANY, ANY, ANY, ANY, VMEM),
         scratch_shapes=[
+            pltpu.VMEM(fine, F32),
+            pltpu.VMEM(fine, F32),
+            pltpu.VMEM(coarse, F32),
+            pltpu.VMEM(coarse, F32),
+            pltpu.VMEM(coarse, F32),
+            pltpu.SMEM((boxes, 6), I32),
+            pltpu.SMEM((1, boxes), I32),
+            pltpu.SMEM((1, 6), I32),
             pltpu.VMEM(fine, F32),
             pltpu.VMEM(fine, F32),
             pltpu.VMEM(coarse, F32),
@@ -1023,7 +1099,8 @@
             pltpu.SemaphoreType.DMA((64,)),
             pltpu.SemaphoreType.DMA,
             pltpu.SemaphoreType.DMA((2, boxes)),
-            pltpu.SemaphoreType.DMA((3,)),
+            pltpu.SemaphoreType.DMA((6,)),
+            pltpu.SemaphoreType.DMA((6,)),
             pltpu.SemaphoreType.DMA((2, boxes // 2, 4)),
             pltpu.SemaphoreType.DMA((2, boxes // 2, 4)),
             pltpu.SemaphoreType.DMA((2, 1, 4)),
@@ -1050,15 +1127,16 @@
     parts = pl.pallas_call(
         functools.partial(bottom_kernel, n_box, n_node, rows_x, rows_y),
         out_shape=like((count, 4, 128)),
-        in_specs=[SMEM, ANY, VMEM],
+        in_specs=[SMEM, ANY, ANY],
         out_specs=VMEM,
         scratch_shapes=[
+            pltpu.VMEM((count, 4, 128), F32),
             pltpu.VMEM((2, deep + 16, wide, 128), F32),
             pltpu.VMEM((2, deep + 16, wide, 128), F32),
             pltpu.VMEM((2, deep + 16, wide, 128), F32),
             pltpu.VMEM((2, deep + 16, wide, 128), F32),
             pltpu.SMEM((count + 1,), I32),
-            pltpu.SemaphoreType.DMA((2,)),
+            pltpu.SemaphoreType.DMA((3,)),
         ],
         compiler_params=pltpu.CompilerParams(vmem_limit_bytes=limit),
         name="bottom",
@@ -1066,9 +1144,20 @@
     fine_out, coarse_out = pl.pallas_call(
         functools.partial(up_kernel, n_box, n_node),
         out_shape=(like(fine), like(coarse)),
-        in_specs=[VMEM, VMEM, VMEM, VMEM, SMEM, SMEM, SMEM, VMEM, VMEM, VMEM, SMEM],
+        in_specs=[ANY, ANY, ANY, ANY, SMEM, ANY, ANY, ANY, ANY, ANY, ANY],
         out_specs=(VMEM, VMEM),
         scratch_shapes=[
+            pltpu.VMEM(fine, F32),
+            pltpu.VMEM(fine, F32),
+            pltpu.VMEM(fine, F32),
+            pltpu.SMEM((boxes, 6), I32),
+            pltpu.SMEM((1, boxes), I32),
+            pltpu.VMEM(coarse, F32),
+            pltpu.VMEM(coarse, F32),
+            pltpu.VMEM(coarse, F32),
+            pltpu.SMEM((1, 6), I32),
+            pltpu.VMEM((chips, 4, 128), F32),
+            pltpu.SemaphoreType.DMA((10,)),
             pltpu.VMEM((chips, 4, 128), F32),
             pltpu.VMEM((chips, 4, 128), F32),
             pltpu.VMEM((chips, 4, 128), F32),

time: 158 us -> 138 us (0.87)
  Pallas kernels: 145 us -> 132 us
  local copies, waits for them, and re-layouts: 10.8 us -> 3.87 us
    pallas_call x1, Pallas kernels: 21.7 us -> 13.3 us  [shards(): pl.pallas_call(functools.partial(bottom_kernel, n_box, n_node, rows_x, ro...]
    unnamed x28 -> x2, local copies, waits for them, and re-layouts: 10.8 us -> 3.87 us
    pallas_call x1, Pallas kernels: 65.6 us -> 61.8 us  [shards(): pl.pallas_call(functools.partial(down_kernel, n_box, n_node), out_shape=(...]
where the time goes in v3:
time: 138 us
  Pallas kernels  132 us (96%)
  local copies, waits for them, and re-layouts  3.87 us (3%)
  between operations  1.95 us (1%)
    pallas_call x1, Pallas kernels, shards(): pl.pallas_call(functools.partial(down_kernel, n_box, n_node), out_shape=(...  61.8 us
    pallas_call x1, Pallas kernels, shards(): pl.pallas_call(functools.partial(up_kernel, n_box, n_node), out_shape=(li...  56.7 us
    pallas_call x1, Pallas kernels, shards(): pl.pallas_call(functools.partial(bottom_kernel, n_box, n_node, rows_x, ro...  13.3 us
    unnamed x2, local copies, waits for them, and re-layouts  3.87 us

profile of v3, /device:TPU:0, one launch (start us, length us, event | category | flops | bytes accessed | tf_op | source)
XLA Modules:
  0.0 137.6 jit_solution(10938398800070922029)
XLA Ops:
  1.9 61.8 %down.1 = (f32[8,32,1024]{2,1,0:T(8,128)}, f32[8,32,1024]{2,1,0:T(8,128)}, f32[1,32,1024]{2,1,0:T(8,128)}, f32[1,32,1024]{2,1,0:T(8,128)}, f32[1,32,1024]{2,1,0:...) custom-call(f32[8,32,1024]{2,1,0:T(8,128)} %fine_b_in.3, f32[8,32,1024]{2,1,0:T(8,128)} %fine_d_in.1, ...), custom_call_target="tpu_custom_call" | custom-call | tf_op jit(solution)/shard_map/down/pallas_call | solution.py:1052
  63.7 13.3 %bottom.1 = f32[128,4,128]{2,1,0:T(4,128)} custom-call(s32[1,128]{1,0:T(1,128)} %get-tuple-element.10.places, f32[30,96,256]{2,1,0:T(8,128)} %get-tuple-element.11.reach, f32[128,4,128]{2,1,0:T(4,128)} %bitcast.3), custom_call_target="tpu_custom_call" | custom-call | tf_op jit(solution)/shard_map/bottom/pallas_call | solution.py:1127
  77.1 56.7 %up.1 = (f32[8,32,1024]{2,1,0:T(8,128)}, f32[1,32,1024]{2,1,0:T(8,128)}) custom-call(f32[2,64,4,128]{3,2,1,0:T(4,128)} %bitcast.2, f32[8,32,1024]{2,1,0:T(8,128)} %get-tuple-element.13.fine_u_in, f32[8,32,1024]{2,1,0:T(8,128)} %get-tuple-element.14.fine_c_in, f32[8,32,1024]{2,1,0:T(8,128)} %fine_b_in.3, s32[1,1]{1,0:T(1,128)S(6)} %copy.14.count_ref, ...), custom_call_target="tpu_custom_call" | custom-call | tf_op jit(solution)/shard_map/up/pallas_call | solution.py:1144
  133.8 2.3 %copy.16 = f32[8,32,1024]{2,1,0:T(8,128)} copy(f32[8,32,1024]{2,1,0:T(8,128)} %get-tuple-element.20) | data formatting | bytes 2097152
  136.1 1.6 %copy.17 = f32[1,32,1024]{2,1,0:T(8,128)} copy(f32[1,32,1024]{2,1,0:T(8,128)} %get-tuple-element.21) | data formatting | bytes 262144

commit v4 on v3

--- a/solution.py
+++ b/solution.py
@@ -68,17 +68,12 @@
         first,
         jnp.where(
             quarter == 1,
-            jnp.where(within < 16, roll_lanes(first, 40), roll_lanes(first, 24)),
-            jnp.where(
-                quarter == 2,
-                jnp.where(within < 16, roll_lanes(last, -24), roll_lanes(last, -40)),
-                last,
-            ),
+            roll_lanes(first, 48),
+            jnp.where(quarter == 2, roll_lanes(last, -16), last),
         ),
     )
     for t in range(TILES):
-        packed = jnp.where(within == t, roll_lanes(tiles[t], t), packed)
-        packed = jnp.where(within == 31 - t, roll_lanes(tiles[t], -t), packed)
+        packed = jnp.where((within >> 1) == t, roll_lanes(tiles[t], 2 * t + 1), packed)
     return packed
 
 
@@ -111,36 +106,54 @@
     )
 
 
-def beside(tiles, ghosts):
-    x_low, x_high, y_low, y_high, z_low, z_high = ghosts
+def beside_inside(tiles):
     lane, row = lanes_of((32, 128)), rows_of((32, 128))
     within = lane & 31
-    below = jnp.where(
-        within < 8,
-        roll_lanes(y_low, 56),
-        jnp.where(within < 24, roll_lanes(y_low, 32), roll_lanes(y_low, 72)),
-    )
-    above = jnp.where(
-        within < 8,
-        roll_lanes(y_high, 56),
-        jnp.where(within < 24, roll_lanes(y_high, 96), roll_lanes(y_high, 72)),
-    )
-    ups = [below] + [roll_lanes(t, 32) for t in tiles]
-    downs = [roll_lanes(t, 96) for t in tiles] + [above]
+    nothing = jnp.zeros((32, 128), F32)
+    ups = [nothing] + [roll_lanes(t, 32) for t in tiles]
+    downs = [roll_lanes(t, 96) for t in tiles] + [nothing]
     sums = []
     for t in range(TILES):
-        cut = slice(128 * t, 128 * (t + 1))
-        along_x = jnp.where(row == 0, x_low[:, cut], pltpu.roll(tiles[t], 1, 0)) + jnp.where(
-            row == 31, x_high[:, cut], pltpu.roll(tiles[t], 31, 0)
+        along_x = jnp.where(row == 0, 0.0, pltpu.roll(tiles[t], 1, 0)) + jnp.where(
+            row == 31, 0.0, pltpu.roll(tiles[t], 31, 0)
         )
         along_y = jnp.where(lane < 32, ups[t], ups[t + 1]) + jnp.where(
             lane >= 96, downs[t + 1], downs[t]
         )
-        along_z = jnp.where(
-            within == 0, roll_lanes(z_low, t - 31), roll_lanes(tiles[t], 1)
-        ) + jnp.where(within == 31, roll_lanes(z_high, 31 - t), roll_lanes(tiles[t], 127))
+        along_z = jnp.where(within == 0, 0.0, roll_lanes(tiles[t], 1)) + jnp.where(
+            within == 31, 0.0, roll_lanes(tiles[t], 127)
+        )
         sums.append(along_x + along_y + along_z)
     return sums
+
+
+def with_ghosts(sums, ghosts):
+    x_low, x_high, y_low, y_high, z_low, z_high = ghosts
+    lane, row = lanes_of((32, 128)), rows_of((8, 128))
+    within = lane & 31
+    below = jnp.where(within < 16, roll_lanes(y_low, 48), roll_lanes(y_low, 32))
+    above = jnp.where(within < 16, roll_lanes(y_high, 48), roll_lanes(y_high, 96))
+    both = jnp.where((lane & 1) == 0, z_low, roll_lanes(z_high, 62))
+    edge = (within == 0) | (within == 31)
+    full = []
+    for t in range(TILES):
+        cut = slice(128 * t, 128 * (t + 1))
+        value = sums[t] + jnp.where(edge, roll_lanes(both, -32 - 2 * t), 0.0)
+        if t == 0:
+            value += jnp.where(lane < 32, below, 0.0)
+        if t == TILES - 1:
+            value += jnp.where(lane >= 96, above, 0.0)
+        full.append(
+            jnp.concatenate(
+                [
+                    value[0:8] + jnp.where(row == 0, x_low[:, cut], 0.0),
+                    value[8:24],
+                    value[24:32] + jnp.where(row == 7, x_high[:, cut], 0.0),
+                ],
+                axis=0,
+            )
+        )
+    return full
 
 
 def fan_out(value, step):
@@ -305,6 +318,25 @@
     lax.fori_loop(0, boxes // step, some, 0)
 
 
+class Store:
+    def __init__(self, source, target, boxes, step, sems):
+        self.source, self.target, self.boxes, self.step = source, target, boxes, step
+        self.sems = sems
+
+    def copy(self, chunk):
+        part = pl.ds(chunk * self.step, self.step)
+        return pltpu.make_async_copy(
+            self.source.at[part], self.target.at[part], self.sems.at[chunk]
+        )
+
+    def start(self, chunk):
+        self.copy(chunk).start()
+
+    def finish(self):
+        for chunk in range(self.boxes // self.step):
+            self.copy(chunk).wait()
+
+
 class Spread:
     def __init__(self, here, source, target, device, send_sems, recv_sems):
         self.here, self.source, self.target, self.device = here, source, target, device
@@ -358,18 +390,28 @@
     by_chunks(boxes, swap, one)
 
 
-def sweep_boxes(boxes, u_ref, b_ref, c_ref, came, nbr_ref, out_ref, swap, keep=None):
-    yz_from, x_from = came.refs
-
+def inside_boxes(boxes, u_ref, b_ref, sum_ref):
     def one(box, carry):
         tiles = tiles_of(u_ref, box)
-        sums = beside(tiles, ghosts_of(yz_from, x_from, nbr_ref, box))
+        sums = beside_inside(tiles)
+        sources = tiles_of(b_ref, box)
+        write_tiles(sum_ref, box, [sources[t] + sums[t] for t in range(TILES)])
+
+    by_chunks(boxes, None, one)
+
+
+def sweep_boxes(
+    boxes, u_ref, sum_ref, c_ref, came, nbr_ref, out_ref, swap, keep=None, store=None
+):
+    yz_from, x_from = came.refs
+
+    def one(box, carry):
+        tiles = tiles_of(u_ref, box)
+        sums = with_ghosts(tiles_of(sum_ref, box), ghosts_of(yz_from, x_from, nbr_ref, box))
         fresh = []
         for t in range(TILES):
             cut = slice(128 * t, 128 * (t + 1))
-            fresh.append(
-                0.2 * tiles[t] + c_ref[box, :, cut] * (b_ref[box, :, cut] + sums[t])
-            )
+            fresh.append(0.2 * tiles[t] + c_ref[box, :, cut] * sums[t])
         if keep is not None:
             kept = keep(box)
             fresh = [t * kept for t in fresh]
@@ -377,19 +419,19 @@
         if swap is not None:
             put_faces(fresh, *swap.refs, boxes + box)
 
-    by_chunks(boxes, swap, one)
-
-
-def residual_boxes(boxes, u_ref, b_ref, d_ref, came, nbr_ref, r_ref, keep=None):
+    by_chunks(boxes, store if swap is None else swap, one)
+
+
+def residual_boxes(boxes, u_ref, sum_ref, d_ref, came, nbr_ref, r_ref, keep=None):
     yz_from, x_from = came.refs
 
     def one(box, carry):
         tiles = tiles_of(u_ref, box)
-        sums = beside(tiles, ghosts_of(yz_from, x_from, nbr_ref, box))
+        sums = with_ghosts(tiles_of(sum_ref, box), ghosts_of(yz_from, x_from, nbr_ref, box))
         rests = []
         for t in range(TILES):
             cut = slice(128 * t, 128 * (t + 1))
-            left = b_ref[box, :, cut] - ((6.0 + d_ref[box, :, cut]) * tiles[t] - sums[t])
+            left = sums[t] - (6.0 + d_ref[box, :, cut]) * tiles[t]
             rests.append(left if keep is None else left * keep(box))
         for t in range(TILES):
             r_ref[pl.ds(pl.multiple_of(box * 32, 32), 32), 128 * t : 128 * (t + 1)] = rests[t]
@@ -432,6 +474,8 @@
     coarse_d,
     bottom_d,
     u_first,
+    fine_sum,
+    coarse_sum,
     yz_fine_0,
     x_fine_0,
     yz_fine_1,
@@ -589,9 +633,10 @@
                 )
             )
 
+    inside_boxes(boxes, u_first, fine_b, fine_sum)
     fine_swaps[0].arrived()
     sweep_boxes(
-        boxes, u_first, fine_b, fine_c, fine_swaps[0], fine_nbr, fine_u, fine_swaps[1]
+        boxes, u_first, fine_sum, fine_c, fine_swaps[0], fine_nbr, fine_u, fine_swaps[1]
     )
     kept.append(keep(fine_u, fine_u_out, 1))
     spreads[0].arrived()
@@ -600,12 +645,13 @@
         (1024, 256), lambda r, l: (r >> 6 == l >> 4) & ((r & 31) >> 1 == (l & 15))
     )
     fold_x = one_hot_of((16 * boxes, 32 * boxes), lambda r, l: l >> 1 == r)
+    inside_boxes(boxes, fine_u, fine_b, fine_sum)
     fine_swaps[1].arrived()
     live = count_ref[0, 0]
     residual_boxes(
         boxes,
         fine_u,
-        fine_b,
+        fine_sum,
         fine_d,
         fine_swaps[1],
         fine_nbr,
@@ -650,16 +696,18 @@
 
     first_sweep(1, cu_first, coarse_b, coarse_d, coarse_c, coarse_swaps[0])
     kept += [keep(coarse_b, coarse_b_out, 2), keep(coarse_c, coarse_c_out, 3)]
+    inside_boxes(1, cu_first, coarse_b, coarse_sum)
     coarse_swaps[0].arrived()
     sweep_boxes(
-        1, cu_first, coarse_b, coarse_c, coarse_swaps[0], coarse_nbr, coarse_u, coarse_swaps[1]
+        1, cu_first, coarse_sum, coarse_c, coarse_swaps[0], coarse_nbr, coarse_u, coarse_swaps[1]
     )
     kept.append(keep(coarse_u, coarse_u_out, 4))
     fold_quarter = one_hot_of(
         (1024, 128), lambda r, l: (r >> 7 == (l >> 3 & 7)) & ((r >> 2 & 7) == ((l & 3) << 1) + (l >> 2 & 1))
     )
+    inside_boxes(1, coarse_u, coarse_b, coarse_sum)
     coarse_swaps[1].arrived()
-    residual_boxes(1, coarse_u, coarse_b, coarse_d, coarse_swaps[1], coarse_nbr, rest_ref)
+    residual_boxes(1, coarse_u, coarse_sum, coarse_d, coarse_swaps[1], coarse_nbr, rest_ref)
     folded = pick_right(rest_ref[0:32], fold_quarter)
     folded = pick_left(one_hot_of((8, 32), lambda r, l: l >> 2 == r), folded) * 0.25
     block = swap_eights(folded)
@@ -851,8 +899,11 @@
     coarse_b_in,
     coarse_c_in,
     coarse_nbr_in,
+    fine_to,
+    coarse_to,
     fine_out,
     coarse_out,
+    output_sems,
     fine_u,
     fine_c,
     fine_b,
@@ -878,6 +929,8 @@
     picked,
     u_first,
     u_second,
+    fine_sum,
+    coarse_sum,
     yz_fine_0,
     x_fine_0,
     yz_fine_1,
@@ -952,18 +1005,22 @@
     cu_first[0] = coarse_u[0] + grown
     put_faces(tiles_of(cu_first, 0), yz_coarse_0, x_coarse_0, 1)
     coarse_swaps[0].start(0)
+    inside_boxes(1, cu_first, coarse_b, coarse_sum)
     coarse_swaps[0].arrived()
     sweep_boxes(
-        1, cu_first, coarse_b, coarse_c, coarse_swaps[0], coarse_nbr, cu_second, coarse_swaps[1]
+        1, cu_first, coarse_sum, coarse_c, coarse_swaps[0], coarse_nbr, cu_second, coarse_swaps[1]
     )
     split = one_hot_of(
         (512, 512),
         lambda r, l: (l >> 8 == (r >> 4 & 1)) & ((l >> 4 & 15) == r >> 5) & ((l & 15) == (r & 15)),
     )
+    inside_boxes(1, cu_second, coarse_b, coarse_sum)
     coarse_swaps[1].arrived()
     sweep_boxes(
-        1, cu_second, coarse_b, coarse_c, coarse_swaps[1], coarse_nbr, coarse_out, None
-    )
+        1, cu_second, coarse_sum, coarse_c, coarse_swaps[1], coarse_nbr, coarse_out, None
+    )
+    coarse_store = Store(coarse_out, coarse_to, 1, 1, output_sems.at[pl.ds(boxes // 2, 1)])
+    coarse_store.start(0)
 
     quarters = jnp.concatenate(
         [
@@ -993,26 +1050,48 @@
         put_faces(tiles_of(u_first, box), yz_fine_0, x_fine_0, boxes + box)
 
     by_chunks(boxes, fine_swaps[0], faces_of)
+    inside_boxes(boxes, u_first, fine_b, fine_sum)
     fine_swaps[0].arrived()
     sweep_boxes(
-        boxes, u_first, fine_b, fine_c, fine_swaps[0], fine_nbr, u_second, fine_swaps[1]
-    )
+        boxes, u_first, fine_sum, fine_c, fine_swaps[0], fine_nbr, u_second, fine_swaps[1]
+    )
+    inside_boxes(boxes, u_second, fine_b, fine_sum)
     fine_swaps[1].arrived()
     live = count_ref[0, 0]
+    fine_store = Store(fine_out, fine_to, boxes, 2, output_sems)
     sweep_boxes(
         boxes,
         u_second,
-        fine_b,
+        fine_sum,
         fine_c,
         fine_swaps[1],
         fine_nbr,
         fine_out,
         None,
         lambda box: jnp.where(box < live, 1.0, 0.0).astype(F32),
+        fine_store,
     )
     copies.finish()
-    for sent in fine_swaps + coarse_swaps + [spread]:
+    for sent in fine_swaps + coarse_swaps + [spread, fine_store, coarse_store]:
         sent.finish()
+
+
+def hand_on_kernel(fine_from, coarse_from, fine_to, coarse_to, fine_held, coarse_held, came, sent):
+    boxes = fine_from.shape[0]
+    paths = [
+        (fine_from.at[box], fine_held.at[box], fine_to.at[box], came.at[box], sent.at[box])
+        for box in range(boxes)
+    ]
+    paths.append((coarse_from, coarse_held, coarse_to, came.at[boxes], sent.at[boxes]))
+    ins = [pltpu.make_async_copy(a, b, sem) for a, b, _, sem, _ in paths]
+    outs = [pltpu.make_async_copy(b, c, sem) for _, b, c, _, sem in paths]
+    for copy in ins:
+        copy.start()
+    for coming, going in zip(ins, outs):
+        coming.wait()
+        going.start()
+    for copy in outs:
+        copy.wait()
 
 
 VMEM, SMEM, ANY = (
@@ -1078,6 +1157,8 @@
             pltpu.VMEM(coarse, F32),
             pltpu.VMEM((rows_x, rows_y, long), F32),
             pltpu.VMEM(fine, F32),
+            pltpu.VMEM(fine, F32),
+            pltpu.VMEM(coarse, F32),
             pltpu.VMEM((3 * boxes, 32, 128), F32),
             pltpu.VMEM((3 * boxes, 2, 1024), F32),
             pltpu.VMEM((3 * boxes, 32, 128), F32),
@@ -1145,8 +1226,11 @@
         functools.partial(up_kernel, n_box, n_node),
         out_shape=(like(fine), like(coarse)),
         in_specs=[ANY, ANY, ANY, ANY, SMEM, ANY, ANY, ANY, ANY, ANY, ANY],
-        out_specs=(VMEM, VMEM),
+        out_specs=(ANY, ANY),
         scratch_shapes=[
+            pltpu.VMEM(fine, F32),
+            pltpu.VMEM(coarse, F32),
+            pltpu.SemaphoreType.DMA((boxes // 2 + 1,)),
             pltpu.VMEM(fine, F32),
             pltpu.VMEM(fine, F32),
             pltpu.VMEM(fine, F32),
@@ -1172,6 +1256,8 @@
             pltpu.VMEM((16 * boxes, 256), F32),
             pltpu.VMEM(fine, F32),
             pltpu.VMEM(fine, F32),
+            pltpu.VMEM(fine, F32),
+            pltpu.VMEM(coarse, F32),
             pltpu.VMEM((3 * boxes, 32, 128), F32),
             pltpu.VMEM((3 * boxes, 2, 1024), F32),
             pltpu.VMEM((3 * boxes, 32, 128), F32),
@@ -1202,7 +1288,20 @@
         coarse_c,
         coarse_nbr,
     )
-    return fine_out, coarse_out
+    return pl.pallas_call(
+        hand_on_kernel,
+        out_shape=(like(fine), like(coarse)),
+        in_specs=[ANY, ANY],
+        out_specs=(ANY, ANY),
+        scratch_shapes=[
+            pltpu.VMEM(fine, F32),
+            pltpu.VMEM(coarse, F32),
+            pltpu.SemaphoreType.DMA((boxes + 1,)),
+            pltpu.SemaphoreType.DMA((boxes + 1,)),
+        ],
+        compiler_params=pltpu.CompilerParams(vmem_limit_bytes=limit),
+        name="hand_on",
+    )(fine_out, coarse_out)
 
 
 def solution(mesh):

time: 138 us -> 132 us (0.957)
  local copies, waits for them, and re-layouts: 3.87 us -> 0 us
  Pallas kernels: 132 us -> 129 us
    pallas_call x1, Pallas kernels: 56.7 us -> 52.8 us  [shards(): pl.pallas_call(functools.partial(up_kernel, n_box, n_node), out_shape=(li...]
    unnamed x2 -> x0, local copies, waits for them, and re-layouts: 3.87 us -> none
    pallas_call x0 -> x1, Pallas kernels: none -> 2.15 us  [shards(): pl.pallas_call(hand_on_kernel, out_shape=(like(fine), like(coarse)), in_s...]
where the time goes in v4:
time: 132 us; the launch traced here: 131 us
  Pallas kernels  129 us (98%)
  between operations  2.11 us (2%)
    pallas_call x1, Pallas kernels, shards(): pl.pallas_call(functools.partial(down_kernel, n_box, n_node), out_shape=(...  60.6 us
    pallas_call x1, Pallas kernels, shards(): pl.pallas_call(functools.partial(up_kernel, n_box, n_node), out_shape=(li...  52.8 us
    pallas_call x1, Pallas kernels, shards(): pl.pallas_call(functools.partial(bottom_kernel, n_box, n_node, rows_x, ro...  13.9 us

profile of v4, /device:TPU:0, one launch (start us, length us, event | category | flops | bytes accessed | tf_op | source)
XLA Modules:
  0.0 131.5 jit_solution(12548063778991916978)
XLA Ops:
  1.9 60.6 %down.1 = (f32[8,32,1024]{2,1,0:T(8,128)}, f32[8,32,1024]{2,1,0:T(8,128)}, f32[1,32,1024]{2,1,0:T(8,128)}, f32[1,32,1024]{2,1,0:T(8,128)}, f32[1,32,1024]{2,1,0:...) custom-call(f32[8,32,1024]{2,1,0:T(8,128)} %fine_b_in.3, f32[8,32,1024]{2,1,0:T(8,128)} %fine_d_in.1, ...), custom_call_target="tpu_custom_call" | custom-call | tf_op jit(solution)/shard_map/down/pallas_call | solution.py:1131
  62.5 13.9 %bottom.1 = f32[128,4,128]{2,1,0:T(4,128)} custom-call(s32[1,128]{1,0:T(1,128)} %get-tuple-element.12.places, f32[30,96,256]{2,1,0:T(8,128)} %get-tuple-element.13.reach, f32[128,4,128]{2,1,0:T(4,128)} %bitcast.3), custom_call_target="tpu_custom_call" | custom-call | tf_op jit(solution)/shard_map/bottom/pallas_call | solution.py:1208
  76.4 52.8 %up.1 = (f32[8,32,1024]{2,1,0:T(8,128)}, f32[1,32,1024]{2,1,0:T(8,128)}) custom-call(f32[2,64,4,128]{3,2,1,0:T(4,128)} %bitcast.2, f32[8,32,1024]{2,1,0:T(8,128)} %get-tuple-element.15.fine_u_in, f32[8,32,1024]{2,1,0:T(8,128)} %get-tuple-element.16.fine_c_in, f32[8,32,1024]{2,1,0:T(8,128)} %fine_b_in.3, s32[1,1]{1,0:T(1,128)S(6)} %copy.12.count_ref, ...), custom_call_target="tpu_custom_call" | custom-call | tf_op jit(solution)/shard_map/up/pallas_call | solution.py:1225
  129.2 2.1 %hand_on.1 = (f32[8,32,1024]{2,1,0:T(8,128)}, f32[1,32,1024]{2,1,0:T(8,128)}) custom-call(f32[8,32,1024]{2,1,0:T(8,128)} %get-tuple-element.20.fine_from, f32[1,32,1024]{2,1,0:T(8,128)} %get-tuple-element.21.coarse_from), custom_call_target="tpu_custom_call" | custom-call | tf_op jit(solution)/shard_map/hand_on/pallas_call | solution.py:1291

commit v5 on v4

--- a/solution.py
+++ b/solution.py
@@ -261,7 +261,7 @@
             )
             return carry
 
-        lax.fori_loop(1, self.chips, chip, 0)
+        lax.fori_loop(1, self.chips, chip, 0, unroll=7)
         self.peer_count = len(peers) + self.chips - 1
 
     def greeted(self):
@@ -338,35 +338,35 @@
 
 
 class Spread:
-    def __init__(self, here, source, target, device, send_sems, recv_sems):
+    def __init__(self, here, source, target, landed, device, send_sem, recv_sem):
         self.here, self.source, self.target, self.device = here, source, target, device
-        self.send_sems, self.recv_sems = send_sems, recv_sems
-
-    def copy(self, step):
+        self.landed, self.send_sem, self.recv_sem = landed, send_sem, recv_sem
+
+    def copy(self, source, target, device):
         return pltpu.make_async_remote_copy(
-            src_ref=self.source(step),
-            dst_ref=self.target(step),
-            send_sem=self.send_sems.at[step],
-            recv_sem=self.recv_sems.at[step],
-            device_id=self.device(step),
+            src_ref=source,
+            dst_ref=target,
+            send_sem=self.send_sem,
+            recv_sem=self.recv_sem,
+            device_id=device,
             device_id_type=MESH,
         )
 
-    def each(self, act):
+    def start(self):
         def one(step, carry):
-            act(self.copy(step))
+            self.copy(self.source(step), self.target(step), self.device(step)).start()
             return carry
 
-        lax.fori_loop(1, self.here.chips, one, 0)
-
-    def start(self):
-        self.each(lambda copy: copy.start())
+        lax.fori_loop(1, self.here.chips, one, 0, unroll=7)
+
+    def whole(self):
+        return self.copy(self.landed, self.landed, self.here.mate())
 
     def arrived(self):
-        self.each(lambda copy: copy.wait_recv())
+        self.whole().wait_recv()
 
     def finish(self):
-        self.each(lambda copy: copy.wait_send())
+        self.whole().wait_send()
 
 
 def write_tiles(ref, box, tiles):
@@ -560,6 +560,7 @@
             here,
             lambda step, ref=ref: ref.at[core, 0],
             lambda step, ref=ref: ref.at[core, step],
+            ref.at[core, pl.ds(1, here.chips - 1)],
             here.at_chip,
             spread_sent.at[number],
             spread_came.at[number],
@@ -584,18 +585,6 @@
     own_copy = pltpu.make_async_copy(slab_c, reach.at[own_x, own_y], local_sem)
     own_copy.start()
     sides_y = (pl.ds(0, Y_HALO), pl.ds(Y_HALO + rows_y, Y_HALO))
-    halo_y = [
-        copies.start(
-            slab_c.at[:, pl.ds(rows_y - Y_HALO, Y_HALO)],
-            reach.at[own_x, sides_y[0]],
-            here.at_node(1),
-        ),
-        copies.start(
-            slab_c.at[:, pl.ds(0, Y_HALO)],
-            reach.at[own_x, sides_y[1]],
-            here.at_node(-1),
-        ),
-    ]
     some = HALO - rows_x
     to_x = (
         (1, 0, rows_x, HALO - rows_x),
@@ -622,16 +611,6 @@
         found_at[target] = slot
 
     own_copy.wait()
-    arrived(halo_y)
-    for step, first, wide, target in to_x:
-        for side in sides_y:
-            halo_x.append(
-                copies.start(
-                    reach.at[pl.ds(HALO + first, wide), side],
-                    reach.at[pl.ds(target, wide), side],
-                    here.at_box(step),
-                )
-            )
 
     inside_boxes(boxes, u_first, fine_b, fine_sum)
     fine_swaps[0].arrived()
@@ -681,6 +660,18 @@
         lambda r, l: (r >> 8 == (l >> 4 & 1)) & ((r >> 4 & 15) == l >> 5) & ((r & 15) == (l & 15)),
     )
     arrived(given)
+    halo_y = [
+        copies.start(
+            slab_c.at[:, pl.ds(rows_y - Y_HALO, Y_HALO)],
+            reach.at[own_x, sides_y[0]],
+            here.at_node(1),
+        ),
+        copies.start(
+            slab_c.at[:, pl.ds(0, Y_HALO)],
+            reach.at[own_x, sides_y[1]],
+            here.at_node(-1),
+        ),
+    ]
     total = placed[pl.ds(pl.multiple_of(here.node * 8, 8), 8)]
     for step in range(n_node - 1):
         total = total + lifted[step]
@@ -706,6 +697,16 @@
         (1024, 128), lambda r, l: (r >> 7 == (l >> 3 & 7)) & ((r >> 2 & 7) == ((l & 3) << 1) + (l >> 2 & 1))
     )
     inside_boxes(1, coarse_u, coarse_b, coarse_sum)
+    arrived(halo_y)
+    for step, first, wide, target in to_x:
+        for side in sides_y:
+            halo_x.append(
+                copies.start(
+                    reach.at[pl.ds(HALO + first, wide), side],
+                    reach.at[pl.ds(target, wide), side],
+                    here.at_box(step),
+                )
+            )
     coarse_swaps[1].arrived()
     residual_boxes(1, coarse_u, coarse_sum, coarse_d, coarse_swaps[1], coarse_nbr, rest_ref)
     folded = pick_right(rest_ref[0:32], fold_quarter)
@@ -987,6 +988,7 @@
         here,
         lambda step: sum_core.at[step],
         lambda step: from_chips.at[step],
+        from_chips.at[pl.ds(1, here.chips - 1)],
         here.before_chip,
         spread_sent,
         spread_came,
@@ -1186,8 +1188,8 @@
             pltpu.SemaphoreType.DMA((2, boxes // 2, 4)),
             pltpu.SemaphoreType.DMA((2, 1, 4)),
             pltpu.SemaphoreType.DMA((2, 1, 4)),
-            pltpu.SemaphoreType.DMA((2, chips)),
-            pltpu.SemaphoreType.DMA((2, chips)),
+            pltpu.SemaphoreType.DMA((2,)),
+            pltpu.SemaphoreType.DMA((2,)),
         ],
         compiler_params=pltpu.CompilerParams(
             collective_id=0, has_side_effects=True, vmem_limit_bytes=limit
@@ -1268,8 +1270,8 @@
             pltpu.SemaphoreType.DMA((2, boxes // 2, 4)),
             pltpu.SemaphoreType.DMA((2, 1, 4)),
             pltpu.SemaphoreType.DMA((2, 1, 4)),
-            pltpu.SemaphoreType.DMA((chips,)),
-            pltpu.SemaphoreType.DMA((chips,)),
+            pltpu.SemaphoreType.DMA,
+            pltpu.SemaphoreType.DMA,
         ],
         compiler_params=pltpu.CompilerParams(
             collective_id=1, has_side_effects=True, vmem_limit_bytes=limit

time: 132 us -> 127 us (0.962)
  Pallas kernels: 129 us -> 125 us
    pallas_call x1, Pallas kernels: 60.6 us -> 58.1 us  [shards(): pl.pallas_call(functools.partial(down_kernel, n_box, n_node), out_shape=(...]
    pallas_call x1, Pallas kernels: 52.8 us -> 50.7 us  [shards(): pl.pallas_call(functools.partial(up_kernel, n_box, n_node), out_shape=(li...]
where the time goes in v5:
time: 127 us
  Pallas kernels  125 us (98%)
  between operations  1.95 us (2%)
    pallas_call x1, Pallas kernels, shards(): pl.pallas_call(functools.partial(down_kernel, n_box, n_node), out_shape=(...  58.1 us
    pallas_call x1, Pallas kernels, shards(): pl.pallas_call(functools.partial(up_kernel, n_box, n_node), out_shape=(li...  50.7 us
    pallas_call x1, Pallas kernels, shards(): pl.pallas_call(functools.partial(bottom_kernel, n_box, n_node, rows_x, ro...  13.7 us

profile of v5, /device:TPU:0, one launch (start us, length us, event | category | flops | bytes accessed | tf_op | source)
XLA Modules:
  0.0 126.6 jit_solution(13216203161713331606)
XLA Ops:
  1.9 58.1 %down.1 = (f32[8,32,1024]{2,1,0:T(8,128)}, f32[8,32,1024]{2,1,0:T(8,128)}, f32[1,32,1024]{2,1,0:T(8,128)}, f32[1,32,1024]{2,1,0:T(8,128)}, f32[1,32,1024]{2,1,0:...) custom-call(f32[8,32,1024]{2,1,0:T(8,128)} %fine_b_in.3, f32[8,32,1024]{2,1,0:T(8,128)} %fine_d_in.1, ...), custom_call_target="tpu_custom_call" | custom-call | tf_op jit(solution)/shard_map/down/pallas_call | solution.py:1133
  60.0 13.7 %bottom.1 = f32[128,4,128]{2,1,0:T(4,128)} custom-call(s32[1,128]{1,0:T(1,128)} %get-tuple-element.12.places, f32[30,96,256]{2,1,0:T(8,128)} %get-tuple-element.13.reach, f32[128,4,128]{2,1,0:T(4,128)} %bitcast.3), custom_call_target="tpu_custom_call" | custom-call | tf_op jit(solution)/shard_map/bottom/pallas_call | solution.py:1210
  73.7 50.7 %up.1 = (f32[8,32,1024]{2,1,0:T(8,128)}, f32[1,32,1024]{2,1,0:T(8,128)}) custom-call(f32[2,64,4,128]{3,2,1,0:T(4,128)} %bitcast.2, f32[8,32,1024]{2,1,0:T(8,128)} %get-tuple-element.15.fine_u_in, f32[8,32,1024]{2,1,0:T(8,128)} %get-tuple-element.16.fine_c_in, f32[8,32,1024]{2,1,0:T(8,128)} %fine_b_in.3, s32[1,1]{1,0:T(1,128)S(6)} %copy.12.count_ref, ...), custom_call_target="tpu_custom_call" | custom-call | tf_op jit(solution)/shard_map/up/pallas_call | solution.py:1227
  124.5 2.1 %hand_on.1 = (f32[8,32,1024]{2,1,0:T(8,128)}, f32[1,32,1024]{2,1,0:T(8,128)}) custom-call(f32[8,32,1024]{2,1,0:T(8,128)} %get-tuple-element.20.fine_from, f32[1,32,1024]{2,1,0:T(8,128)} %get-tuple-element.21.coarse_from), custom_call_target="tpu_custom_call" | custom-call | tf_op jit(solution)/shard_map/hand_on/pallas_call | solution.py:1293

commit v6 on v5

--- a/solution.py
+++ b/solution.py
@@ -205,7 +205,8 @@
         self.n_box, self.n_node = n_box, n_node
         self.ny, self.nz, self.nc = grid_of(n_box)
         self.box, self.node = lax.axis_index("box"), lax.axis_index("node")
-        self.chips = self.ny * self.nz * n_node
+        self.line, self.sheet = self.nc * n_node, self.ny * self.nz
+        self.chips = self.sheet * n_node
         self.core = self.box & 1
         self.z = (self.box >> 1) & (self.nz - 1)
         self.y = (self.box >> 1) >> (self.nz.bit_length() - 1)
@@ -227,13 +228,16 @@
     def mate(self):
         return (self.box ^ 1, self.node)
 
-    def at_chip(self, step):
+    def at_line(self, step, sign):
         x_bits = self.n_node.bit_length() - 1
+        x = (self.node + sign * (step & self.n_node - 1)) & (self.n_node - 1)
+        return (self.box ^ (step >> x_bits), x)
+
+    def at_sheet(self, step, sign):
         z_bits = self.nz.bit_length() - 1
-        x = (self.node + step) & (self.n_node - 1)
-        z = (self.z + (step >> x_bits)) & (self.nz - 1)
-        y = (self.y + (step >> x_bits + z_bits)) & (self.ny - 1)
-        return ((y * self.nz + z) * self.nc + self.core, x)
+        z = (self.z + sign * (step & self.nz - 1)) & (self.nz - 1)
+        y = (self.y + sign * (step >> z_bits)) & (self.ny - 1)
+        return ((y * self.nz + z) * self.nc + self.core, self.node)
 
     def before_chip(self, step):
         x_bits = self.n_node.bit_length() - 1
@@ -247,22 +251,20 @@
         for step in range(1, self.n_node):
             yield self.next_node(step), self.at_node(step)
 
-    def greet(self, more):
+    def greet(self, more, all_chips=False):
         peers = [self.along_line(1), self.along_line(-1)] + more
-        peers += [device for _, device in self.peers_node()]
-        peers.append(self.mate())
         barrier = pltpu.get_barrier_semaphore()
         for device in peers:
             pl.semaphore_signal(barrier, inc=1, device_id=device, device_id_type=MESH)
 
         def chip(step, carry):
-            pl.semaphore_signal(
-                barrier, inc=1, device_id=self.at_chip(step), device_id_type=MESH
-            )
+            device = self.before_chip(step)
+            pl.semaphore_signal(barrier, inc=1, device_id=device, device_id_type=MESH)
             return carry
 
-        lax.fori_loop(1, self.chips, chip, 0, unroll=7)
-        self.peer_count = len(peers) + self.chips - 1
+        if all_chips:
+            lax.fori_loop(1, self.chips, chip, 0, unroll=7)
+        self.peer_count = len(peers) + (self.chips - 1 if all_chips else 0)
 
     def greeted(self):
         pl.semaphore_wait(pltpu.get_barrier_semaphore(), self.peer_count)
@@ -338,8 +340,8 @@
 
 
 class Spread:
-    def __init__(self, here, source, target, landed, device, send_sem, recv_sem):
-        self.here, self.source, self.target, self.device = here, source, target, device
+    def __init__(self, count, source, target, landed, device, send_sem, recv_sem):
+        self.count, self.source, self.target, self.device = count, source, target, device
         self.landed, self.send_sem, self.recv_sem = landed, send_sem, recv_sem
 
     def copy(self, source, target, device):
@@ -357,16 +359,39 @@
             self.copy(self.source(step), self.target(step), self.device(step)).start()
             return carry
 
-        lax.fori_loop(1, self.here.chips, one, 0, unroll=7)
+        lax.fori_loop(1, self.count, one, 0, unroll=7 if self.count > 16 else self.count - 1)
 
     def whole(self):
-        return self.copy(self.landed, self.landed, self.here.mate())
+        return self.copy(self.landed, self.landed, self.device(1))
 
     def arrived(self):
         self.whole().wait_recv()
 
     def finish(self):
         self.whole().wait_send()
+
+
+def write_to_all(here, ref, send_sems, recv_sems):
+    return (
+        Spread(
+            here.line,
+            lambda step: ref.at[0, 0],
+            lambda step: ref.at[0, step],
+            ref.at[0, pl.ds(1, here.line - 1)],
+            lambda step: here.at_line(step, 1),
+            send_sems.at[0],
+            recv_sems.at[0],
+        ),
+        Spread(
+            here.sheet,
+            lambda step: ref.at[0],
+            lambda step: ref.at[step],
+            ref.at[pl.ds(1, here.sheet - 1)],
+            lambda step: here.at_sheet(step, 1),
+            send_sems.at[1],
+            recv_sems.at[1],
+        ),
+    )
 
 
 def write_tiles(ref, box, tiles):
@@ -532,7 +557,11 @@
     ]
     for copy in inputs:
         copy.start()
-    here.greet([here.at_box(1), here.at_box(-1), here.at_box(2), here.at_box(-2)])
+    here.greet(
+        [here.at_box(step) for step in (1, -1, 2, -2)]
+        + [here.at_line(step, 1) for step in range(1, here.line)]
+        + [here.at_sheet(step, 1) for step in range(1, here.sheet)]
+    )
 
     def keep(source, target, number):
         copy = pltpu.make_async_copy(source, target, output_sems.at[number])
@@ -543,8 +572,7 @@
         fine_input(box, 0).wait()
         fine_input(box, 1).wait()
 
-    core = here.core
-    places[core, 0] = jnp.full((1, 128), place_ref[0], I32)
+    places[0, 0] = jnp.full((1, 128), place_ref[0], I32)
     fine_swaps = [
         Swap(here, yz, x, boxes, step, fine_sent.at[number], fine_came.at[number])
         for number, (yz, x, step) in enumerate(
@@ -555,18 +583,8 @@
         Swap(here, yz, x, 1, 1, coarse_sent.at[number], coarse_came.at[number])
         for number, (yz, x) in enumerate(((yz_coarse_0, x_coarse_0), (yz_coarse_1, x_coarse_1)))
     ]
-    spreads = [
-        Spread(
-            here,
-            lambda step, ref=ref: ref.at[core, 0],
-            lambda step, ref=ref: ref.at[core, step],
-            ref.at[core, pl.ds(1, here.chips - 1)],
-            here.at_chip,
-            spread_sent.at[number],
-            spread_came.at[number],
-        )
-        for number, ref in enumerate((places, blocks))
-    ]
+    place_spreads = write_to_all(here, places, spread_sent.at[0], spread_came.at[0])
+    block_spreads = write_to_all(here, blocks, spread_sent.at[1], spread_came.at[1])
 
     first_sweep(boxes, u_first, fine_b, fine_d, fine_c, fine_swaps[0], ready)
     kept = [keep(fine_c, fine_c_out, 0)]
@@ -600,7 +618,7 @@
         )
         for step, first, wide, target in to_x
     ]
-    spreads[0].start()
+    place_spreads[0].start()
 
     for copy in inputs[1:]:
         copy.wait()
@@ -618,8 +636,8 @@
         boxes, u_first, fine_sum, fine_c, fine_swaps[0], fine_nbr, fine_u, fine_swaps[1]
     )
     kept.append(keep(fine_u, fine_u_out, 1))
-    spreads[0].arrived()
-    mate_places = copies.start(places.at[core], places.at[core], here.mate())
+    place_spreads[0].arrived()
+    place_spreads[1].start()
     fold_yz = one_hot_of(
         (1024, 256), lambda r, l: (r >> 6 == l >> 4) & ((r & 31) >> 1 == (l & 15))
     )
@@ -713,23 +731,24 @@
     folded = pick_left(one_hot_of((8, 32), lambda r, l: l >> 2 == r), folded) * 0.25
     block = swap_eights(folded)
     late = pltpu.roll(block, 64, 1)
-    blocks[core, 0] = jnp.where(lanes_of((4, 128)) < 64, block[0:4], late[4:8])
-
-    spreads[1].start()
-    arrived([mate_places])
+    blocks[0, 0] = jnp.where(lanes_of((4, 128)) < 64, block[0:4], late[4:8])
+
+    block_spreads[0].start()
+    place_spreads[1].arrived()
+    block_spreads[0].arrived()
+    block_spreads[1].start()
     row = jnp.zeros((1, 128), I32)
     lane = lanes_of((1, 128))
     for number in range(n_box * n_node):
-        row = jnp.where(lane == number, places[number // here.chips, number % here.chips], row)
+        row = jnp.where(lane == number, places[number // here.line, number % here.line], row)
     places_out[...] = row
-    spreads[1].arrived()
-    arrived([copies.start(blocks.at[core], blocks.at[core], here.mate())])
+    block_spreads[1].arrived()
     kept.append(keep(blocks, blocks_out, 5))
     arrived(halo_x)
     copies.finish()
     for copy in kept:
         copy.wait()
-    for sent in fine_swaps + coarse_swaps + spreads:
+    for sent in fine_swaps + coarse_swaps + [*place_spreads, *block_spreads]:
         sent.finish()
 
 
@@ -948,12 +967,11 @@
     here = Place(n_box, n_node)
     copies = Copies(send_sems, recv_sems)
     boxes = fine_u.shape[0]
-    core = here.core
     inputs = [
         pltpu.make_async_copy(source, target, input_sems.at[number])
         for number, (source, target) in enumerate(
             (
-                (parts_in.at[core], own_parts),
+                (parts_in.at[:, pl.ds(0, n_node)], own_parts),
                 (coarse_u_in, coarse_u),
                 (coarse_b_in, coarse_b),
                 (coarse_c_in, coarse_c),
@@ -976,24 +994,25 @@
         Swap(here, yz, x, 1, 1, coarse_sent.at[number], coarse_came.at[number])
         for number, (yz, x) in enumerate(((yz_coarse_0, x_coarse_0), (yz_coarse_1, x_coarse_1)))
     ]
-    here.greet([])
+    here.greet([here.mate()], True)
     here.greeted()
 
-    from_mate = copies.start(parts_in.at[1 - core], from_core, here.mate())
+    from_mate = copies.start(parts_in.at[:, pl.ds(n_node, n_node)], from_core, here.mate())
     for copy in inputs:
         copy.wait()
     arrived([from_mate])
     sum_core[...] = own_parts[...] + from_core[...]
+    x_bits = n_node.bit_length() - 1
     spread = Spread(
-        here,
-        lambda step: sum_core.at[step],
+        here.chips,
+        lambda step: sum_core.at[step >> x_bits, step & n_node - 1],
         lambda step: from_chips.at[step],
         from_chips.at[pl.ds(1, here.chips - 1)],
         here.before_chip,
         spread_sent,
         spread_came,
     )
-    from_chips[0] = sum_core[0]
+    from_chips[0] = sum_core[0, 0]
     spread.start()
     grow_quarter = one_hot_of(
         (128, 1024), lambda r, l: r == (l >> 7 << 3) + (l >> 3 & 3) + (l >> 2 & 1) * 4
@@ -1127,8 +1146,8 @@
         return jax.ShapeDtypeStruct(shape, kind)
 
     fine, coarse = (boxes, 32, 1024), (1, 32, 1024)
-    chips = ny * nz * n_node
-    grid = (nc, chips)
+    line = nc * n_node
+    grid = (ny * nz, line)
     limit = 62 * 1024 * 1024
     fine_u, fine_c, coarse_u, coarse_b, coarse_c, reach, blocks, places = pl.pallas_call(
         functools.partial(down_kernel, n_box, n_node),
@@ -1188,8 +1207,8 @@
             pltpu.SemaphoreType.DMA((2, boxes // 2, 4)),
             pltpu.SemaphoreType.DMA((2, 1, 4)),
             pltpu.SemaphoreType.DMA((2, 1, 4)),
-            pltpu.SemaphoreType.DMA((2,)),
-            pltpu.SemaphoreType.DMA((2,)),
+            pltpu.SemaphoreType.DMA((2, 2)),
+            pltpu.SemaphoreType.DMA((2, 2)),
         ],
         compiler_params=pltpu.CompilerParams(
             collective_id=0, has_side_effects=True, vmem_limit_bytes=limit
@@ -1242,11 +1261,11 @@
             pltpu.VMEM(coarse, F32),
             pltpu.VMEM(coarse, F32),
             pltpu.SMEM((1, 6), I32),
-            pltpu.VMEM((chips, 4, 128), F32),
+            pltpu.VMEM((ny * nz, n_node, 4, 128), F32),
             pltpu.SemaphoreType.DMA((10,)),
-            pltpu.VMEM((chips, 4, 128), F32),
-            pltpu.VMEM((chips, 4, 128), F32),
-            pltpu.VMEM((chips, 4, 128), F32),
+            pltpu.VMEM((ny * nz, n_node, 4, 128), F32),
+            pltpu.VMEM((ny * nz, n_node, 4, 128), F32),
+            pltpu.VMEM((ny * nz * n_node, 4, 128), F32),
             pltpu.VMEM((8, 128), F32),
             pltpu.VMEM(coarse, F32),
             pltpu.VMEM(coarse, F32),

time: 127 us -> 126 us (level)
  Pallas kernels: 125 us -> 123 us
    pallas_call x1, Pallas kernels: 50.7 us -> 49.1 us  [shards(): pl.pallas_call(functools.partial(up_kernel, n_box, n_node), out_shape=(li...]
where the time goes in v6:
time: 126 us; the launch traced here: 125 us
  Pallas kernels  123 us (98%)
  between operations  2.11 us (2%)
    pallas_call x1, Pallas kernels, shards(): pl.pallas_call(functools.partial(down_kernel, n_box, n_node), out_shape=(...  58 us
    pallas_call x1, Pallas kernels, shards(): pl.pallas_call(functools.partial(up_kernel, n_box, n_node), out_shape=(li...  49.1 us
    pallas_call x1, Pallas kernels, shards(): pl.pallas_call(functools.partial(bottom_kernel, n_box, n_node, rows_x, ro...  13.8 us

profile of v6, /device:TPU:0, one launch (start us, length us, event | category | flops | bytes accessed | tf_op | source)
XLA Modules:
  0.0 125.2 jit_solution(3939614130529779581)
XLA Ops:
  1.9 58.0 %down.1 = (f32[8,32,1024]{2,1,0:T(8,128)}, f32[8,32,1024]{2,1,0:T(8,128)}, f32[1,32,1024]{2,1,0:T(8,128)}, f32[1,32,1024]{2,1,0:T(8,128)}, f32[1,32,1024]{2,1,0:...) custom-call(f32[8,32,1024]{2,1,0:T(8,128)} %fine_b_in.3, f32[8,32,1024]{2,1,0:T(8,128)} %fine_d_in.1, ...), custom_call_target="tpu_custom_call" | custom-call | tf_op jit(solution)/shard_map/down/pallas_call | solution.py:1152
  60.0 13.8 %bottom.1 = f32[128,4,128]{2,1,0:T(4,128)} custom-call(s32[1,128]{1,0:T(1,128)} %get-tuple-element.12.places, f32[30,96,256]{2,1,0:T(8,128)} %get-tuple-element.13.reach, f32[128,4,128]{2,1,0:T(4,128)} %bitcast.3), custom_call_target="tpu_custom_call" | custom-call | tf_op jit(solution)/shard_map/bottom/pallas_call | solution.py:1229
  73.8 49.1 %up.1 = (f32[8,32,1024]{2,1,0:T(8,128)}, f32[1,32,1024]{2,1,0:T(8,128)}) custom-call(f32[16,8,4,128]{3,2,1,0:T(4,128)} %bitcast.2, f32[8,32,1024]{2,1,0:T(8,128)} %get-tuple-element.15.fine_u_in, f32[8,32,1024]{2,1,0:T(8,128)} %get-tuple-element.16.fine_c_in, f32[8,32,1024]{2,1,0:T(8,128)} %fine_b_in.3, s32[1,1]{1,0:T(1,128)S(6)} %copy.12.count_ref, ...), custom_call_target="tpu_custom_call" | custom-call | tf_op jit(solution)/shard_map/up/pallas_call | solution.py:1246
  122.9 2.1 %hand_on.1 = (f32[8,32,1024]{2,1,0:T(8,128)}, f32[1,32,1024]{2,1,0:T(8,128)}) custom-call(f32[8,32,1024]{2,1,0:T(8,128)} %get-tuple-element.20.fine_from, f32[1,32,1024]{2,1,0:T(8,128)} %get-tuple-element.21.coarse_from), custom_call_target="tpu_custom_call" | custom-call | tf_op jit(solution)/shard_map/hand_on/pallas_call | solution.py:1312

commit v7 on v6

--- a/solution.py
+++ b/solution.py
@@ -12,7 +12,7 @@
 BOT_ITERS = 12
 HALO = BOT_ITERS - 1
 Y_HALO = 16
-AT_ONCE = 4
+AT_ONCE = 6
 TILES = 8
 
 
@@ -587,6 +587,8 @@
     block_spreads = write_to_all(here, blocks, spread_sent.at[1], spread_came.at[1])
 
     first_sweep(boxes, u_first, fine_b, fine_d, fine_c, fine_swaps[0], ready)
+    here.greeted()
+    fine_swaps[0].start(0)
     kept = [keep(fine_c, fine_c_out, 0)]
     rows_x, rows_y = bottom_d.shape[0], bottom_d.shape[1]
     inputs[0].wait()
@@ -597,8 +599,6 @@
         return carry
 
     lax.fori_loop(0, rows_x, scale_plane, 0)
-    here.greeted()
-    fine_swaps[0].start(0)
     own_x, own_y = pl.ds(HALO, rows_x), pl.ds(Y_HALO, rows_y)
     own_copy = pltpu.make_async_copy(slab_c, reach.at[own_x, own_y], local_sem)
     own_copy.start()

time: 126 us -> 126 us (level)
    pallas_call x1, Pallas kernels: 49.1 us -> 52.1 us  [shards(): pl.pallas_call(functools.partial(up_kernel, n_box, n_node), out_shape=(li...]
    pallas_call x1, Pallas kernels: 58 us -> 56.3 us  [shards(): pl.pallas_call(functools.partial(down_kernel, n_box, n_node), out_shape=(...]
where the time goes in v7:
time: 126 us
  Pallas kernels  124 us (98%)
  between operations  2.11 us (2%)
    pallas_call x1, Pallas kernels, shards(): pl.pallas_call(functools.partial(down_kernel, n_box, n_node), out_shape=(...  56.3 us
    pallas_call x1, Pallas kernels, shards(): pl.pallas_call(functools.partial(up_kernel, n_box, n_node), out_shape=(li...  52.1 us
    pallas_call x1, Pallas kernels, shards(): pl.pallas_call(functools.partial(bottom_kernel, n_box, n_node, rows_x, ro...  13.5 us

profile of v7, /device:TPU:0, one launch (start us, length us, event | category | flops | bytes accessed | tf_op | source)
XLA Modules:
  0.0 126.1 jit_solution(14458171668916468490)
XLA Ops:
  1.9 56.3 %down.1 = (f32[8,32,1024]{2,1,0:T(8,128)}, f32[8,32,1024]{2,1,0:T(8,128)}, f32[1,32,1024]{2,1,0:T(8,128)}, f32[1,32,1024]{2,1,0:T(8,128)}, f32[1,32,1024]{2,1,0:...) custom-call(f32[8,32,1024]{2,1,0:T(8,128)} %fine_b_in.3, f32[8,32,1024]{2,1,0:T(8,128)} %fine_d_in.1, ...), custom_call_target="tpu_custom_call" | custom-call | tf_op jit(solution)/shard_map/down/pallas_call | solution.py:1152
  58.2 13.5 %bottom.1 = f32[128,4,128]{2,1,0:T(4,128)} custom-call(s32[1,128]{1,0:T(1,128)} %get-tuple-element.12.places, f32[30,96,256]{2,1,0:T(8,128)} %get-tuple-element.13.reach, f32[128,4,128]{2,1,0:T(4,128)} %bitcast.3), custom_call_target="tpu_custom_call" | custom-call | tf_op jit(solution)/shard_map/bottom/pallas_call | solution.py:1229
  71.7 52.1 %up.1 = (f32[8,32,1024]{2,1,0:T(8,128)}, f32[1,32,1024]{2,1,0:T(8,128)}) custom-call(f32[16,8,4,128]{3,2,1,0:T(4,128)} %bitcast.2, f32[8,32,1024]{2,1,0:T(8,128)} %get-tuple-element.15.fine_u_in, f32[8,32,1024]{2,1,0:T(8,128)} %get-tuple-element.16.fine_c_in, f32[8,32,1024]{2,1,0:T(8,128)} %fine_b_in.3, s32[1,1]{1,0:T(1,128)S(6)} %copy.12.count_ref, ...), custom_call_target="tpu_custom_call" | custom-call | tf_op jit(solution)/shard_map/up/pallas_call | solution.py:1246
  123.8 2.1 %hand_on.1 = (f32[8,32,1024]{2,1,0:T(8,128)}, f32[1,32,1024]{2,1,0:T(8,128)}) custom-call(f32[8,32,1024]{2,1,0:T(8,128)} %get-tuple-element.20.fine_from, f32[1,32,1024]{2,1,0:T(8,128)} %get-tuple-element.21.coarse_from), custom_call_target="tpu_custom_call" | custom-call | tf_op jit(solution)/shard_map/hand_on/pallas_call | solution.py:1312
